TPU v7x, 32 devices: a whole 2x2x4 slice. The times are simulated.
32 devices in a mesh: seq: 8 (over y, x, core), row: 4 (over z).
Axes of the slice: x: 2, y: 2, z: 4, core: 2. Of those that a mesh axis runs over, the one named last changes fastest.
Arguments:
- block_input: bfloat16 [16, 1024, 512], P('row', 'seq'), may hold values from -6 to 6
- segment_ids: int32 [16, 1024], P('row'), may hold values from 0 to 1, as said below
- ln1_gain: float32 [512], replicated, may hold values from 0.5 to 1.5
- ln1_shift: float32 [512], replicated, may hold values from -1.5 to 1.5
- w_qkv: bfloat16 [512, 1536], replicated, may hold values from -0.375 to 0.375
- bias_query: float32 [512], replicated, may hold values from -1.5 to 1.5
- bias_value: float32 [512], replicated, may hold values from -1.5 to 1.5
- w_out: bfloat16 [512, 512], replicated, may hold values from -1 to 1
- bias_out: float32 [512], replicated, may hold values from -1.5 to 1.5
- ln2_gain: float32 [512], replicated, may hold values from 0.5 to 1.5
- ln2_shift: float32 [512], replicated, may hold values from -1.5 to 1.5
- w_up: bfloat16 [512, 2048], replicated, may hold values from -0.25 to 0.25
- bias_up: float32 [2048], replicated, may hold values from -1.5 to 1.5
- w_down: bfloat16 [2048, 512], replicated, may hold values from -0.125 to 0.125
- bias_down: float32 [512], replicated, may hold values from -1.5 to 1.5
- out_grad: bfloat16 [16, 1024, 512], P('row', 'seq'), may hold values from -6 to 6
Outputs:
- output: bfloat16 [16, 1024, 512], P('row', 'seq')
- input_grad: bfloat16 [16, 1024, 512], P('row', 'seq')
- grad_ln1_gain: float32 [512], replicated
- grad_ln1_shift: float32 [512], replicated
- grad_w_qkv: float32 [512, 1536], replicated
- grad_bias_query: float32 [512], replicated
- grad_bias_value: float32 [512], replicated
- grad_w_out: float32 [512, 512], replicated
- grad_bias_out: float32 [512], replicated
- grad_ln2_gain: float32 [512], replicated
- grad_ln2_shift: float32 [512], replicated
- grad_w_up: float32 [512, 2048], replicated
- grad_bias_up: float32 [2048], replicated
- grad_w_down: float32 [2048, 512], replicated
- grad_bias_down: float32 [512], replicated
Inputs may be any that keep to these rules, and one draw needn't show every extreme that they name: `segment_ids`: ids start at 0 and never fall along a row, rising by one at each new crop; equal ids mark one crop, whose tokens attend only to each other; in each aligned group of 4 rows one row, drawn from the seed, is a single crop, and every other row holds exactly 1024 // (4 * 128) crops.
All inputs are finite; a program needn't handle non-finite values.
Results may differ from a plain program's by a relative error of at most 0.015.
Values may be sent and summed in bfloat16 or wider, within the bound.
No kernel may reach another device: no remote copies, remote signals or barrier semaphores. Data moves between devices by JAX's collectives and lax.ppermute only.
A program may use at most 256 MiB of HBM per device.

v0:
```python
import functools

import jax
import jax.numpy as jnp
from jax import lax
from jax.experimental import pallas as pl
from jax.experimental.pallas import tpu as pltpu
from jax.sharding import PartitionSpec as P

HEADS = 8
EPSILON = 1e-06
BIG = 1e30
LSE_LANE = 16
PIECES = 16
AT_ONCE = 2
SCHEDULE = (
    "U", "D", "u", "b", "u", "b", "u", "d", "G", "u", "q", "d", "u", "L", "q", "d",
    "u", "q", "d", "q", "u", "d", "O", "q", "d", "u", "q", "d", "q", "I", "u", "d",
    "q", "d", "q",
)
MODES = {"d": "xy", "u": "xy", "q": "xy"}
VECTOR_LANES = 128
F32 = jnp.float32
BF16 = jnp.bfloat16
MIB = 1024 * 1024
LN1_GAIN, LN1_SHIFT, BIAS_Q, BIAS_V, BIAS_OUT, LN2_GAIN, LN2_SHIFT, BIAS_DOWN = (
    slice(i, i + 1) for i in range(8)
)
BIAS_UP = 8


def dot_nn(a, b):
    return lax.dot_general(a, b, (((1,), (0,)), ((), ())), preferred_element_type=F32)


def dot_nt(a, b):
    return lax.dot_general(a, b, (((1,), (1,)), ((), ())), preferred_element_type=F32)


def dot_tn(a, b):
    return lax.dot_general(a, b, (((0,), (0,)), ((), ())), preferred_element_type=F32)


def split_three(value):
    high = value.astype(BF16)
    rest = value - high.astype(F32)
    middle = rest.astype(BF16)
    low = (rest - middle.astype(F32)).astype(BF16)
    return high, middle, low


def lane_index(shape):
    return lax.broadcasted_iota(jnp.int32, shape, len(shape) - 1)


def three_lanes(value, lanes):
    high, middle, low = split_three(value)
    spot = lanes % 64
    out = jnp.where(spot == LSE_LANE, high.astype(F32), 0.0)
    out = jnp.where(spot == LSE_LANE + 1, middle.astype(F32), out)
    return jnp.where(spot == LSE_LANE + 2, low.astype(F32), out)


def norm_parts(value):
    centre = jnp.mean(value, axis=-1, keepdims=True)
    centred = value - centre
    spread = jnp.mean(centred * centred, axis=-1, keepdims=True)
    scale = lax.rsqrt(spread + EPSILON)
    return centred * scale, scale


def norm_back(grad, unit, scale, gain):
    grad_unit = grad * gain
    first = jnp.mean(grad_unit, axis=-1, keepdims=True)
    second = jnp.mean(grad_unit * unit, axis=-1, keepdims=True)
    return scale * (grad_unit - first - unit * second)


def fetch_kernel(source, target, sem):
    copy = pltpu.make_async_copy(source, target, sem)
    copy.start()
    copy.wait()


def fetch(array):
    return pl.pallas_call(
        fetch_kernel,
        in_specs=[pl.BlockSpec(memory_space=pl.ANY)],
        out_specs=vmem(),
        out_shape=jax.ShapeDtypeStruct(array.shape, array.dtype),
        scratch_shapes=[pltpu.SemaphoreType.DMA],
        compiler_params=pltpu.CompilerParams(vmem_limit_bytes=8 * MIB),
        name="fetch",
    )(array)


def qkv_kernel(pieces, width, *refs):
    x_refs = refs[:pieces]
    small, w_ref, x_ref, normed_ref, q_ref, kv_ref = refs[pieces:]
    band = x_refs[0].shape[0]
    for j in range(pieces):
        x_ref[j * band : (j + 1) * band, :] = x_refs[j][...]
        unit, _ = norm_parts(x_refs[j][...].astype(F32))
        normed_ref[j * band : (j + 1) * band, :] = (unit * small[LN1_GAIN] + small[LN1_SHIFT]).astype(BF16)
    normed = normed_ref[...]
    q = dot_nn(normed, w_ref[:, :width])
    q_ref[...] = ((q + small[BIAS_Q]) * (width // HEADS) ** -0.5).astype(BF16)
    kv_ref[:, :width] = dot_nn(normed, w_ref[:, width : 2 * width]).astype(BF16)
    kv_ref[:, width:] = (dot_nn(normed, w_ref[:, 2 * width :]) + small[BIAS_V]).astype(BF16)


def forward_kernel(parts, wide, rows, *refs):
    q_ref = refs[0]
    k_refs = refs[1 : 1 + parts]
    v_refs = refs[1 + parts : 1 + 2 * parts]
    qf_ref, kf_ref, mix_ref, qfb_ref, k_aug, v_aug = refs[1 + 2 * parts :]
    tokens = q_ref.shape[0]
    low_half = (lane_index((1, 128)) < 64).astype(F32)
    halves = (low_half.astype(BF16), (1.0 - low_half).astype(BF16))
    for pair in range(wide):
        at = slice(128 * pair, 128 * (pair + 1))
        for parity in range(2):
            mine, other = halves[parity], halves[1 - parity]
            start = 0
            for k_ref, v_ref in zip(k_refs, v_refs):
                stop = start + k_ref.shape[0]
                k_aug[2 * pair + parity, start:stop, :] = k_ref[:, at] * mine + kf_ref[start:stop, :] * other
                v_aug[2 * pair + parity, start:stop, :] = v_ref[:, at] * mine + other
                start = stop
    lanes = lane_index((rows, 128))
    low = lanes < 64
    held = {}

    def scores_of(pair, block, parity):
        at, heads = slice(block * rows, (block + 1) * rows), slice(128 * pair, 128 * (pair + 1))
        q = q_ref[at, heads] * halves[parity] + qf_ref[at, :] * halves[1 - parity]
        return dot_nt(q, k_aug[2 * pair + parity])

    def use(pair, block, parity, scores):
        top = jnp.max(scores, axis=-1, keepdims=True)
        exps = jnp.exp(scores - top).astype(BF16)
        sums = dot_nn(exps, v_aug[2 * pair + parity])
        if parity == 0:
            held[0] = (sums, top)
            return
        (even, even_top), odd, odd_top = held[0], sums, top
        at, heads = slice(block * rows, (block + 1) * rows), slice(128 * pair, 128 * (pair + 1))
        total = jnp.where(low, odd, even)
        mix_ref[at, heads] = jnp.where(low, even, odd) / pltpu.roll(total, 64, 1)
        log_total = jnp.where(low, odd_top, even_top) + jnp.log(total)
        qfb_ref[at, heads] = (qf_ref[at, :].astype(F32) + three_lanes(-log_total, lanes)).astype(BF16)

    before = None
    for pair in range(wide):
        for block in range(tokens // rows):
            for parity in range(2):
                now = (pair, block, parity, scores_of(pair, block, parity))
                if before is not None:
                    use(*before)
                before = now
    use(*before)


def attention_forward(q, kvs, qf, kf, wide=2, rows=256):
    tokens, width = q.shape
    lanes = 128 * wide
    steps = width // lanes
    length = kf.shape[0]
    parts = len(kvs)
    in_specs = [pl.BlockSpec((tokens, lanes), lambda h: (0, h))]
    in_specs += [pl.BlockSpec((kv.shape[0], lanes), lambda h: (0, h)) for kv in kvs]
    in_specs += [pl.BlockSpec((kv.shape[0], lanes), lambda h: (0, steps + h)) for kv in kvs]
    in_specs += [
        pl.BlockSpec((tokens, 128), lambda h: (0, 0)),
        pl.BlockSpec((length, 128), lambda h: (0, 0)),
    ]
    return pl.pallas_call(
        functools.partial(forward_kernel, parts, wide, rows),
        grid=(steps,),
        in_specs=in_specs,
        out_specs=[
            pl.BlockSpec((tokens, lanes), lambda h: (0, h)),
            pl.BlockSpec((tokens, lanes), lambda h: (0, h)),
        ],
        out_shape=[
            jax.ShapeDtypeStruct((tokens, width), F32),
            jax.ShapeDtypeStruct((tokens, width), BF16),
        ],
        scratch_shapes=[pltpu.VMEM((2 * wide, length, 128), BF16), pltpu.VMEM((2 * wide, length, 128), BF16)],
        compiler_params=pltpu.CompilerParams(vmem_limit_bytes=(8 + 8 * length // 1024) * MIB),
        name="attention_forward",
        cost_estimate=pl.CostEstimate(
            flops=4 * tokens * length * width, bytes_accessed=8 * tokens * width,
            transcendentals=tokens * length * HEADS,
        ),
    )(q, *kvs, *kvs, qf, kf)


def backward_kernel(parts, count, rows, *refs):
    q_ref, gm_ref, qfb_ref, gmf_ref = refs[:4]
    k_refs = refs[4 : 4 + parts]
    v_refs = refs[4 + parts : 4 + 2 * parts]
    kf_ref = refs[4 + 2 * parts]
    rest = refs[5 + 2 * parts :]
    dq_ref = rest[0]
    pair_refs = rest[1 : 1 + parts]
    q_aug, gm_aug, dqt = rest[1 + parts :]
    low_half = (lane_index((1, 128)) < 64).astype(F32)
    halves = (low_half.astype(BF16), (1.0 - low_half).astype(BF16))
    low = lane_index((rows, 128)) < 64
    for pair in range(count):
        heads = slice(128 * pair, 128 * (pair + 1))
        for parity in range(2):
            mine, other = halves[parity], halves[1 - parity]
            q_aug[2 * pair + parity] = q_ref[:, heads] * mine + qfb_ref[:, heads] * other
            gm_aug[2 * pair + parity] = gm_ref[:, heads] * mine + gmf_ref[:, heads] * other
        start = 0
        for k_ref, v_ref, pair_ref in zip(k_refs, v_refs, pair_refs):
            for block in range(k_ref.shape[0] // rows):
                at = slice(block * rows, (block + 1) * rows)
                k, v = k_ref[at, heads], v_ref[at, heads]
                kf = kf_ref[start + block * rows : start + (block + 1) * rows, :]
                dks, dvs = [], []
                for parity in range(2):
                    mine, other = halves[parity], halves[1 - parity]
                    probs = jnp.exp(dot_nt(k * mine + kf * other, q_aug[2 * pair + parity]))
                    slopes = dot_nt(v * mine + other, gm_aug[2 * pair + parity])
                    grads = (probs * slopes).astype(BF16)
                    dvs.append(dot_nn(probs.astype(BF16), gm_ref[:, heads]))
                    dks.append(dot_nn(grads, q_ref[:, heads]))
                    term = dot_tn(k, grads)
                    if start + block == 0:
                        dqt[2 * pair + parity] = term
                    else:
                        dqt[2 * pair + parity] += term
                left, right = 256 * pair, 256 * pair + 128
                pair_ref[at, left:right] = jnp.where(low, dks[0], dks[1]).astype(pair_ref.dtype)
                pair_ref[at, right : right + 128] = jnp.where(low, dvs[0], dvs[1]).astype(pair_ref.dtype)
            start += k_ref.shape[0]
        dq_t = jnp.concatenate([dqt[2 * pair, :64, :], dqt[2 * pair + 1, 64:, :]], axis=0)
        dq_ref[:, heads] = dq_t.T.astype(BF16) * (64.0**-0.5)


def attention_backward(q, gm, qfb, gmf, kvs, kf, first, count, rows=512):
    tokens, width = q.shape
    length = kf.shape[0]
    parts = len(kvs)
    lanes = 128 * count
    steps = width // lanes
    own = lambda i: (0, first // count)
    in_specs = [pl.BlockSpec((tokens, lanes), own)] * 4
    in_specs += [pl.BlockSpec((kv.shape[0], lanes), own) for kv in kvs]
    in_specs += [pl.BlockSpec((kv.shape[0], lanes), lambda i: (0, steps + first // count)) for kv in kvs]
    in_specs += [pl.BlockSpec((length, 128), lambda i: (0, 0))]
    kinds = [F32] + [BF16] * (parts - 1)
    outs = [jax.ShapeDtypeStruct((tokens, 128 * count), BF16)]
    outs += [jax.ShapeDtypeStruct((kv.shape[0], 256 * count), kind) for kv, kind in zip(kvs, kinds)]
    return pl.pallas_call(
        functools.partial(backward_kernel, parts, count, rows),
        grid=(1,),
        in_specs=in_specs,
        out_specs=[pl.BlockSpec(out.shape, lambda i: (0, 0)) for out in outs],
        out_shape=outs,
        scratch_shapes=[
            pltpu.VMEM((2 * count, tokens, 128), BF16),
            pltpu.VMEM((2 * count, tokens, 128), BF16),
            pltpu.VMEM((2 * count, 128, tokens), F32),
        ],
        compiler_params=pltpu.CompilerParams(vmem_limit_bytes=(12 + 4 * length // 1024) * MIB),
        name="attention_backward",
        cost_estimate=pl.CostEstimate(
            flops=10 * tokens * length * 128 * count, bytes_accessed=12 * tokens * 128 * count,
            transcendentals=tokens * length * 2 * count,
        ),
    )(q, gm, qfb, gmf, *kvs, *kvs, kf)


def middle_kernel(pieces, rows, *refs):
    dy_refs = refs[:pieces]
    x_ref, mix_ref, small, w_out, w_up, w_down = refs[pieces : pieces + 6]
    outs = refs[pieces + 6 :]
    gain, shift = small[LN2_GAIN], small[LN2_SHIFT]
    out_refs = outs[:pieces]
    (mixed_ref, two_ref, active_ref, gh_ref, ga_ref, gmid_ref, gm_ref, gmf_ref, vec_ref, dy_ref) = outs[pieces:]
    band = dy_refs[0].shape[0]
    tokens, width = mix_ref.shape
    ff = w_up.shape[1]
    vec_ref[...] = jnp.zeros_like(vec_ref)
    c0 = 0.7978845608028654
    c1 = 0.044715
    row = lax.broadcasted_iota(jnp.int32, (width, width), 0) // 64
    column = lane_index((width, width)) // 64
    opposite = (row == (column + 1 - 2 * (column % 2))).astype(F32).astype(BF16)
    per = rows // band
    for t in range(tokens // rows):
        at = slice(t * rows, (t + 1) * rows)
        x = x_ref[at, :].astype(F32)
        dy = jnp.concatenate([dy_refs[t * per + j][...] for j in range(per)], axis=0)
        dy_ref[at, :] = dy
        mix = mix_ref[at, :]
        mixed = mix.astype(BF16)
        mixed_ref[at, :] = mixed
        middle = x + (dot_nn(mixed, w_out[...]) + small[BIAS_OUT])
        unit, scale = norm_parts(middle)
        two = (unit * gain + shift).astype(BF16)
        two_ref[at, :] = two
        out = middle + small[BIAS_DOWN]
        grad_two = jnp.zeros((rows, width), F32)
        step = 2 * width
        before = None
        for f in range(0, ff + step, step):
            if f < ff:
                fs = slice(f, f + step)
                bias = jnp.concatenate(
                    [small[BIAS_UP + i : BIAS_UP + i + 1] for i in range(f // width, (f + step) // width)], axis=1
                )
                now = (fs, dot_nn(two, w_up[:, fs]) + bias, dot_nt(dy, w_down[fs, :]))
            if before is not None:
                fs, hidden, grad = before
                square = hidden * hidden
                tanh = jnp.tanh(c0 * hidden * (1.0 + c1 * square))
                half = 0.5 * (1.0 + tanh)
                active = (hidden * half).astype(BF16)
                active_ref[at, fs] = active
                out = out + dot_nn(active, w_down[fs, :])
                slope = half + hidden * (0.5 * (1.0 - tanh * tanh)) * (c0 + (3.0 * c0 * c1) * square)
                grad_low = (grad * slope).astype(BF16)
                gh_ref[at, fs] = grad_low
                vec_ref[0:1, fs] += jnp.sum(grad_low.astype(F32), axis=0, keepdims=True)
                grad_two = grad_two + dot_nt(grad_low, w_up[:, fs])
            before = now
        for j in range(per):
            out_refs[t * per + j][...] = out[j * band : (j + 1) * band].astype(BF16)
        dy_wide = dy.astype(F32)
        grad_middle = dy_wide + norm_back(grad_two, unit, scale, gain)
        gmid_ref[at, :] = grad_middle
        vec_ref[1:2, :width] += jnp.sum(grad_two * unit, axis=0, keepdims=True)
        vec_ref[2:3, :width] += jnp.sum(grad_two, axis=0, keepdims=True)
        vec_ref[3:4, :width] += jnp.sum(dy_wide, axis=0, keepdims=True)
        grad_attn = grad_middle.astype(BF16)
        ga_ref[at, :] = grad_attn
        vec_ref[4:5, :width] += jnp.sum(grad_attn.astype(F32), axis=0, keepdims=True)
        gm = dot_nt(grad_attn, w_out[...]).astype(BF16)
        gm_ref[at, :] = gm
        high, mid, _ = split_three(gm.astype(F32) * mix)
        inner = dot_nn(high, opposite) + dot_nn(mid, opposite)
        gmf_ref[at, :] = three_lanes(-inner, lane_index((rows, width))).astype(BF16)


def middle_part(dys, x, mix, small, w_out, w_up, w_down, rows=512):
    tokens, width = mix.shape
    ff = w_up.shape[1]
    shape = jax.ShapeDtypeStruct
    return pl.pallas_call(
        functools.partial(middle_kernel, len(dys), rows),
        out_shape=[shape(dy.shape, BF16) for dy in dys]
        + [
            shape((tokens, width), BF16),
            shape((tokens, width), BF16),
            shape((tokens, ff), BF16),
            shape((tokens, ff), BF16),
            shape((tokens, width), BF16),
            shape((tokens, width), F32),
            shape((tokens, width), BF16),
            shape((tokens, width), BF16),
            shape((8, ff), F32),
            shape((tokens, width), BF16),
        ],
        compiler_params=pltpu.CompilerParams(vmem_limit_bytes=24 * MIB),
        name="middle_part",
        cost_estimate=pl.CostEstimate(
            flops=2 * tokens * width * (4 * ff + 5 * width), bytes_accessed=8 * 1024 * 1024,
            transcendentals=tokens * ff,
        ),
    )(*dys, x, mix, small, w_out, w_up, w_down)


def columns_by_way(mode, columns):
    middle = columns // 256 * 128
    return {
        "x": ((0, columns, 0),),
        "y": ((0, columns, 1),),
        "xy": ((0, middle, 0), (middle, columns, 1)),
    }[mode]


def place_pieces(marks, mode, total, keep_ref, send_ref):
    piece = total.shape[0] // PIECES
    for which, target in enumerate((keep_ref, send_ref)):
        for start, stop, way in columns_by_way(mode, total.shape[1]):

            def move(j, carry, which=which, target=target, start=start, stop=stop, way=way):
                source = pl.ds(pl.multiple_of((marks[2 * which + way] ^ j) * piece, piece), piece)
                spot = pl.ds(pl.multiple_of(j * piece, piece), piece)
                target[spot, start:stop] = total[source, start:stop].astype(BF16)
                return carry

            lax.fori_loop(0, PIECES // 2, move, 0)


def smem():
    return pl.BlockSpec(memory_space=pltpu.SMEM)


def vmem():
    return pl.BlockSpec(memory_space=pltpu.VMEM)


def weight_grad_kernel(count, mode, marks, *refs):
    pairs = refs[: 2 * count]
    keep_ref, send_ref, total = refs[2 * count :]
    start = 0
    for left, right in zip(pairs[0::2], pairs[1::2]):
        stop = start + right.shape[1]
        for r in range(0, left.shape[1], 256):
            total[r : r + 256, start:stop] = dot_tn(left[:, r : r + 256], right[...])
        start = stop
    place_pieces(marks, mode, total, keep_ref, send_ref)


def weight_grad(marks, mode, pairs, name):
    rows = pairs[0][0].shape[1]
    columns = sum(right.shape[1] for _, right in pairs)
    depth = pairs[0][0].shape[0]
    half = jax.ShapeDtypeStruct((rows // 2, columns), BF16)
    flat = [array for pair in pairs for array in pair]
    return pl.pallas_call(
        functools.partial(weight_grad_kernel, len(pairs), mode),
        in_specs=[smem()] + [vmem()] * len(flat),
        out_specs=[vmem(), vmem()],
        out_shape=[half, half],
        scratch_shapes=[pltpu.VMEM((rows, columns), F32)],
        compiler_params=pltpu.CompilerParams(vmem_limit_bytes=16 * MIB),
        name=name,
        cost_estimate=pl.CostEstimate(
            flops=2 * rows * columns * depth, bytes_accessed=6 * rows * columns, transcendentals=0
        ),
    )(marks, *flat)


def qkv_grad_kernel(count, mode, *refs):
    marks, normed, small, w_ref, vec_ref = refs[:5]
    dqs, owns, gots = (refs[5 + i * count : 5 + (i + 1) * count] for i in range(3))
    packed, keep_ref, send_ref, total = refs[5 + 3 * count :]
    width = normed.shape[1]
    share = width // count
    for t in range(count):
        packed[:, share * t : share * (t + 1)] = dqs[t][...]
        both = (owns[t][...] + gots[t][...].astype(F32)).astype(BF16)
        for i in range(2 * share // 128):
            at = (i % 2 + 1) * width + share * t + 128 * (i // 2)
            packed[:, at : at + 128] = both[:, 128 * i : 128 * (i + 1)]
    for r in range(0, width, 256):
        total[r : r + 256, : 3 * width] = dot_tn(normed[:, r : r + 256], packed[...])
    sums = jnp.sum(packed[...].astype(F32), axis=0, keepdims=True)
    terms = jnp.concatenate(split_three(jnp.broadcast_to(sums, (16, 3 * width))), axis=0)
    spread = dot_nt(terms, w_ref[...])
    shift_row = spread[0:1] + (spread[16:17] + spread[32:33])
    rows = jnp.zeros((width, 128), F32)
    for at in range(0, 3 * width, 128):
        rows = rows + total[:, at : at + 128] * w_ref[:, at : at + 128].astype(F32)
    gain_row = jnp.sum(rows.T, axis=0, keepdims=True)
    gain_row = (gain_row - small[LN1_SHIFT] * shift_row) / small[LN1_GAIN]
    vectors = [vec_ref[0:1, :]] + [vec_ref[i : i + 1, :width] for i in range(1, 5)]
    vectors += [sums[:, :width], sums[:, 2 * width :], gain_row, shift_row]
    tiles = [row[:, at : at + VECTOR_LANES] for row in vectors for at in range(0, row.shape[1], VECTOR_LANES)]
    piece = width // PIECES
    per = len(tiles) // PIECES
    total[:, 3 * width :] = jnp.zeros((width, VECTOR_LANES), F32)
    for i, tile in enumerate(tiles):
        at = (i // per) * piece + i % per
        total[at : at + 1, 3 * width :] = tile
    place_pieces(marks, mode, total, keep_ref, send_ref)


def qkv_grad(marks, mode, normed, small, w_qkv, vec, dqs, owns, gots):
    tokens, width = normed.shape
    columns = 3 * width + VECTOR_LANES
    half = jax.ShapeDtypeStruct((width // 2, columns), BF16)
    flat = [normed, small, w_qkv, vec, *dqs, *owns, *gots]
    return pl.pallas_call(
        functools.partial(qkv_grad_kernel, len(dqs), mode),
        in_specs=[smem()] + [vmem()] * len(flat),
        out_specs=[vmem()] * 3,
        out_shape=[jax.ShapeDtypeStruct((tokens, 3 * width), BF16), half, half],
        scratch_shapes=[pltpu.VMEM((width, columns), F32)],
        compiler_params=pltpu.CompilerParams(vmem_limit_bytes=16 * MIB),
        name="qkv_grad",
        cost_estimate=pl.CostEstimate(
            flops=6 * tokens * width * width, bytes_accessed=18 * tokens * width, transcendentals=0
        ),
    )(marks, *flat)


def last_kernel(pieces, packed, gmid_ref, small, w_ref, x_ref, *out_refs):
    band = out_refs[0].shape[0]
    grad = dot_nt(packed[...], w_ref[...])
    unit, scale = norm_parts(x_ref[...].astype(F32))
    result = (gmid_ref[...] + norm_back(grad, unit, scale, small[LN1_GAIN])).astype(BF16)
    for j in range(pieces):
        out_refs[j][...] = result[j * band : (j + 1) * band]


def last_part(packed, gmid, small, w_qkv, x, pieces):
    tokens, width = gmid.shape
    return pl.pallas_call(
        functools.partial(last_kernel, pieces),
        out_shape=[jax.ShapeDtypeStruct((tokens // pieces, width), BF16)] * pieces,
        compiler_params=pltpu.CompilerParams(vmem_limit_bytes=12 * MIB),
        name="last_part",
        cost_estimate=pl.CostEstimate(
            flops=6 * tokens * width * width, bytes_accessed=10 * tokens * width, transcendentals=0
        ),
    )(packed, gmid, small, w_qkv, x)


def assemble_kernel(segments, mode, per, marks, *refs):
    own_far, out_refs = refs[:2], refs[2:]
    half = PIECES // 2
    piece = own_far[0].shape[0] // half
    step = pl.program_id(0)

    def one(i, carry):
        index = step * per + i

        def fill(which):
            source = own_far[which]
            for low, high, way in columns_by_way(mode, source.shape[1]):
                at = pl.ds(pl.multiple_of(((index ^ marks[2 * which + way]) % half) * piece, piece), piece)
                for start, stop, which_out, tall, offset in segments:
                    first, last = max(start, low), min(stop, high)
                    if first < last:
                        spot = pl.ds(pl.multiple_of(i * tall + offset, piece), piece)
                        out_refs[which_out][spot, first - start : last - start] = source[at, first:last].astype(F32)

        mine = index // half == marks[0] // half
        pl.when(mine)(functools.partial(fill, 0))
        pl.when(jnp.logical_not(mine))(functools.partial(fill, 1))
        return carry

    lax.fori_loop(0, per, one, 0)


def assemble(marks, mode, parts, segments, shapes, name):
    steps = 2
    per = PIECES // steps
    size = sum(rows * columns for rows, columns in shapes)
    return pl.pallas_call(
        functools.partial(assemble_kernel, segments, mode, per),
        grid=(steps,),
        in_specs=[smem()] + [vmem()] * 2,
        out_specs=[pl.BlockSpec((rows // steps, w), lambda i: (i, 0)) for rows, w in shapes],
        out_shape=[jax.ShapeDtypeStruct(shape, F32) for shape in shapes],
        compiler_params=pltpu.CompilerParams(vmem_limit_bytes=16 * MIB),
        name=name,
        cost_estimate=pl.CostEstimate(flops=size, bytes_accessed=6 * size, transcendentals=0),
    )(marks, *parts)


def return_kernel(halves, row_ref, *refs):
    out, sems = refs[-2], refs[-1]
    copies = []
    for i, (ref, (j, half)) in enumerate(zip(refs, halves)):
        width = ref.shape[1]
        at = 0 if half is None else half * width
        copies.append(pltpu.make_async_copy(ref, out.at[row_ref[0] ^ j, :, at : at + width], sems.at[i]))
    for copy in copies:
        copy.start()
    for copy in copies:
        copy.wait()


def return_rows(row, own, halves, name):
    flat = [own] + [piece for half in halves for piece in half]
    places = [(0, None)] + [(j + 1, h) for h, half in enumerate(halves) for j in range(len(half))]
    pieces = len(halves[0]) + 1
    return pl.pallas_call(
        functools.partial(return_kernel, places),
        in_specs=[smem()] + [vmem()] * len(flat),
        out_specs=pl.BlockSpec(memory_space=pl.ANY),
        out_shape=jax.ShapeDtypeStruct((pieces, *own.shape), BF16),
        scratch_shapes=[pltpu.SemaphoreType.DMA((len(flat),))],
        compiler_params=pltpu.CompilerParams(vmem_limit_bytes=4 * MIB),
        name=name,
    )(row, *flat)


def swap(value, axis, size, mask):
    return lax.ppermute(value, axis, [(i, i ^ mask) for i in range(size)])


class Order:
    def __init__(self):
        self.last = ()

    def enter(self, *values):
        return lax.optimization_barrier((values, self.last))[0]

    def leave(self, *values):
        self.last = values


class Cargo:
    def __init__(self, pieces):
        self.pieces = pieces
        width = pieces[0].shape[1] // 2
        self.columns = [slice(0, width), slice(width, 2 * width)]
        self.came = [[None] * len(pieces) for _ in range(2)]
        self.onward = [None, None]

    def load(self, half, way, first):
        columns = self.columns[half]
        far = self.pieces[3][:, columns] if first else self.onward[half]
        return jnp.concatenate([self.pieces[way + 1][:, columns], far], axis=0)

    def land(self, half, way, first, got):
        band = got.shape[0] // 2
        self.came[half][way + 1] = got[:band]
        if first:
            self.onward[half] = got[band:]
        else:
            self.came[half][3] = got[band:]


def fold(value, rows):
    if rows < value.shape[0]:
        return jnp.concatenate([value[at : at + rows] for at in range(0, value.shape[0], rows)], axis=1)
    wide = value.shape[1] * value.shape[0] // rows
    return jnp.concatenate([value[:, at : at + wide] for at in range(0, value.shape[1], wide)], axis=0)


class Wave:
    def __init__(self, order, keep, send, marks, mode, layout, core, ways, deep, rest):
        self.order, self.core, self.ways, self.deep, self.rest = order, core, ways, deep, rest
        self.marks, self.mode, self.layout = marks, mode, layout
        self.parts = columns_by_way(mode, keep.shape[1])
        self.value, self.got = [keep], [core(send)]
        self.cargo, self.aboard = {}, None
        order.leave(send)

    def arrived(self):
        count = len(self.value)
        values = self.order.enter(*self.value, *self.got)
        kept, came = values[:count], list(values[count:])
        if self.aboard is not None:
            cargo, first, ways, shape = self.aboard
            for i, way in enumerate(ways):
                own = self.parts[i][1] - self.parts[i][0]
                cargo.land(i, way, first, fold(came[i][:, own:], shape[0]))
                came[i] = came[i][:, :own]
            self.aboard = None
        return list(zip(kept, came))

    def added(self):
        return [add_low(one, two) for one, two in self.arrived()]

    def split(self, value):
        return [value[:, start:stop] for start, stop, _ in self.parts]

    def travel(self, step, values, key):
        ways = [(step + way) % 2 for _, _, way in self.parts]
        if key in self.cargo:
            cargo, first = self.cargo[key]
            loads = [cargo.load(i, way, first) for i, way in enumerate(ways)]
            self.aboard = (cargo, first, ways, loads[0].shape)
            values = [
                jnp.concatenate([value, fold(load, value.shape[0])], axis=1) for value, load in zip(values, loads)
            ]
        self.got = [self.ways[way](value) for way, value in zip(ways, values)]
        self.order.leave(*values)

    def plane(self, step):
        values = self.added()
        if step == 0:
            values = self.split(values[0])
        half = values[0].shape[0] // 2
        self.value = [value[:half] for value in values]
        self.travel(step, [value[half:] for value in values], ("out", step))

    def line(self):
        values = self.added()
        half = values[0].shape[0] // 2
        self.value = [jnp.concatenate([value[:half] for value in values], axis=1)]
        sent = jnp.concatenate([value[half:] for value in values], axis=1)
        self.got = [self.deep(sent)]
        self.order.leave(sent)

    def exchanges(self):
        for send in self.rest:
            self.value = self.added()
            self.got = [send(self.value[0])]
            self.order.leave(*self.value)

    def line_back(self):
        self.value = self.added()
        self.got = [self.deep(self.value[0])]
        self.order.leave(*self.value)

    def joined(self):
        return [jnp.concatenate(pair, axis=0) for pair in self.arrived()]

    def plane_back(self, step):
        values = self.joined()
        self.value = self.split(values[0]) if step == 1 else values
        self.travel(step, self.value, ("back", step))

    def core_back(self):
        self.value = [jnp.concatenate(self.joined(), axis=1)]
        self.got = [self.core(self.value[0])]
        self.order.leave(*self.value)

    def wait(self):
        self.got = list(self.order.enter(*self.got))
        self.order.leave(*self.got)

    def finish(self):
        ((own, far),) = self.arrived()
        self.sums = assemble(self.marks, self.mode, (own, far), *self.layout)
        self.order.leave(*self.sums)

    def steps(self):
        yield functools.partial(self.plane, 0)
        yield functools.partial(self.plane, 1)
        yield self.line
        yield self.exchanges
        yield self.line_back
        yield functools.partial(self.plane_back, 1)
        yield functools.partial(self.plane_back, 0)
        yield self.core_back
        yield self.finish


def add_low(one, two):
    return (one.astype(F32) + two.astype(F32)).astype(BF16)


def after(value, *others):
    return lax.optimization_barrier((value, others))[0]


def bits_of(axis, size):
    found, mask = [], 1
    while mask < size:
        found.append((axis, size, mask, (lax.axis_index(axis) // mask) % 2))
        mask *= 2
    return found


def per_device(
    seq_size, row_size,
    block_input, segment_ids, ln1_gain, ln1_shift, w_qkv, bias_query, bias_value, w_out, bias_out,
    ln2_gain, ln2_shift, w_up, bias_up, w_down, bias_down, out_grad,
):
    rows, band, width = block_input.shape
    length = segment_ids.shape[1]
    share = seq_size // rows
    tokens = rows * band
    crops = max(length // (4 * band), 1)
    place = lax.axis_index("seq")
    my_row, my_part = place // share, place % share

    def deal(pieces):
        got = [pieces[0]]
        for j in range(1, rows):
            turn = [(s, ((s // share) ^ j) * share + s % share) for s in range(seq_size)]
            got.append(lax.ppermute(pieces[j], "seq", turn))
        return got

    def pick(array):
        return [lax.dynamic_index_in_dim(array, my_row ^ j, 0, False) for j in range(rows)]

    xs = deal(pick(block_input))
    dys = pick(out_grad)

    own_row = lax.dynamic_index_in_dim(segment_ids, my_row, 0, False).reshape(seq_size, band)
    key_ids = jnp.concatenate(
        [
            lax.dynamic_index_in_dim(own_row, (my_row ^ j) * share + (my_part ^ i), 0, False)
            for i in range(share)
            for j in range(rows)
        ]
    )
    spot = jnp.arange(128) % 64
    same = key_ids[:, None] == spot[None, :]
    used = spot[None, :] < crops
    ones = (spot >= LSE_LANE) & (spot < LSE_LANE + 3)
    kf = jnp.where(used, jnp.where(same, 0.0, -1.0), jnp.where(ones, 1.0, 0.0)).astype(BF16)
    qf = jnp.where(used & same, BIG, 0.0).astype(BF16)[:tokens]

    small = jnp.stack(
        [ln1_gain, ln1_shift, bias_query, bias_value, bias_out, ln2_gain, ln2_shift, bias_down]
    )
    small = jnp.concatenate([small, bias_up.reshape(-1, width)], axis=0)
    shape = jax.ShapeDtypeStruct
    x, normed, q, kv = pl.pallas_call(
        functools.partial(qkv_kernel, rows, width),
        out_shape=[
            shape((tokens, width), BF16),
            shape((tokens, width), BF16),
            shape((tokens, width), BF16),
            shape((tokens, 2 * width), BF16),
        ],
        compiler_params=pltpu.CompilerParams(vmem_limit_bytes=12 * MIB),
        name="norm_and_project",
    )(*xs, small, w_qkv)


    dys = list(lax.optimization_barrier((dys, kv))[0])
    dys = deal(dys)
    seq_bits = bits_of("seq", seq_size)
    row_bits = bits_of("row", row_size)
    part_bits = [bit for bit in seq_bits if bit[2] < share]
    kvs, whole = [kv], kv
    for axis, size, mask, own in part_bits:
        got = swap(whole, axis, size, mask)
        kvs.append(got)
        if mask * 2 < share:
            whole = jnp.concatenate([whole, got], 0)

    mix, qfb = attention_forward(q, kvs, qf, kf)
    *outs, mixed, two, active, grad_hidden, grad_attn, grad_middle, gm, gmf, vec, dy = middle_part(
        dys, x, mix, small, w_out, w_up, w_down
    )

    def straight(bit):
        return lambda value: swap(value, *bit[:3])

    plane = [bit for bit in seq_bits if bit[2] >= share]
    core, one, two_, deep = seq_bits[0][3], plane[0][3], plane[1][3], row_bits[0][3]
    ways = (straight(plane[0]), straight(plane[1]))
    rest = [straight(bit) for bit in row_bits[1:] + plane[2:] + part_bits[1:]]
    route = (straight(seq_bits[0]), ways, straight(row_bits[0]), rest)
    left, right = one * 4 + two_ * 2 + deep, two_ * 4 + one * 2 + deep
    mine, other = core * 8, 8 - core * 8
    marks = jnp.stack([mine + left, mine + right, other + left, other + right]).astype(jnp.int32)

    pairs = width // 128
    ff = w_up.shape[1]
    tall = width // PIECES
    down_layout = ([(0, width, 0, ff // PIECES, 0)], [(ff, width)], "assemble_down")
    up_segments = [(0, ff, 0, tall, 0), (ff, ff + width, 1, tall, 0)]
    up_layout = (up_segments, [(width, ff), (width, width)], "assemble_up_out")
    qkv_segments = [(0, 3 * width, 0, tall, 0), (3 * width, 3 * width + VECTOR_LANES, 1, tall, 0)]
    qkv_layout = (qkv_segments, [(width, 3 * width), (width, VECTOR_LANES)], "assemble_qkv")
    row = my_row.astype(jnp.int32).reshape(1)

    order = Order()
    terms, gots, steps, done = [], [], {}, {}

    def backward():
        (grad,) = order.enter(gm)
        terms.append(attention_backward(q, grad, qfb, gmf, kvs, kf, AT_ONCE * len(terms), AT_ONCE))
        order.leave(*terms[-1])
        if share == 2:
            gots.append(straight(part_bits[0])(terms[-1][2]))

    def start_wave(letter, pairs_of, name, layout):
        flat = order.enter(*[array for pair in pairs_of for array in pair])
        keep, send = weight_grad(marks, MODES[letter], list(zip(flat[0::2], flat[1::2])), name)
        done[letter] = Wave(order, keep, send, marks, MODES[letter], layout, *route)
        steps[letter] = done[letter].steps()
        if letter == "d":
            ride("d", outs, "out", "o")

    def start_qkv():
        own_terms, far_terms = [term[1] for term in terms], gots
        if share != 2:
            both = jnp.concatenate(
                [jnp.concatenate([part.astype(BF16) for part in term[1:]], 0) for term in terms], axis=1
            )
            for bit in reversed(part_bits):
                half = both.shape[0] // 2
                kept, got = both[:half], straight(bit)(both[half:])
                both = add_low(kept, got)
            cuts = [slice(256 * AT_ONCE * t, 256 * AT_ONCE * (t + 1)) for t in range(len(terms))]
            own_terms = [kept[:, cut].astype(F32) for cut in cuts]
            far_terms = [got[:, cut] for cut in cuts]
        (vec_,) = order.enter(vec)
        dqs = [term[0] for term in terms]
        done["p"], keep, send = qkv_grad(marks, MODES["q"], normed, small, w_qkv, vec_, dqs, own_terms, far_terms)
        done["q"] = Wave(order, keep, send, marks, MODES["q"], qkv_layout, *route)
        steps["q"] = done["q"].steps()

    def last():
        (packed,) = order.enter(done["p"])
        pieces = last_part(packed, grad_middle, small, w_qkv, x, rows)
        order.leave(*pieces)
        ride("u", pieces, "back", "i")

    def ride(letter, pieces, stage, name):
        done[name] = Cargo(pieces)
        steps_ = (0, 1) if stage == "out" else (1, 0)
        for i, step in enumerate(steps_):
            done[letter].cargo[(stage, step)] = (done[name], i == 0)

    def take_back(name):
        cargo = done[name]
        halves = [list(order.enter(*half[1:])) for half in cargo.came]
        done[name] = return_rows(row, cargo.pieces[0], halves, "return_rows")
        order.leave(done[name])

    actions = {
        "b": backward,
        "D": lambda: start_wave("d", [(active, dy)], "grad_down", down_layout),
        "U": lambda: start_wave("u", [(two, grad_hidden), (mixed, grad_attn)], "grad_up_out", up_layout),
        "G": start_qkv,
        "L": last,
        "O": lambda: take_back("o"),
        "I": lambda: take_back("i"),
        "d": lambda: next(steps["d"])(),
        "u": lambda: next(steps["u"])(),
        "q": lambda: next(steps["q"])(),
    }
    def wait(which):
        if which.isdigit():
            if share == 2:
                (gots[int(which)],) = order.enter(gots[int(which)])
                order.leave(gots[int(which)])
        else:
            done[which].wait()

    for word in SCHEDULE:
        if word[0] == "w":
            wait(word[1])
        else:
            actions[word]()
    result, input_grad = done["o"], done["i"]
    (sum_down,) = done["d"].sums
    sum_up, sum_out = done["u"].sums
    sum_qkv, tiles = done["q"].sums

    count = (ff + 8 * width) // VECTOR_LANES // PIECES
    vectors = tiles.reshape(PIECES, -1, VECTOR_LANES)[:, :count].reshape(-1)
    cuts = [ff + i * width for i in range(9)]
    names = [vectors[a:b] for a, b in zip(cuts[:-1], cuts[1:])]
    ln2_gain_sum, ln2_shift_sum, bias_down_sum, bias_out_sum = names[:4]
    bias_q_sum, bias_v_sum, ln1_gain_sum, ln1_shift_sum = names[4:]
    return (
        result,
        input_grad,
        ln1_gain_sum,
        ln1_shift_sum,
        sum_qkv,
        bias_q_sum,
        bias_v_sum,
        sum_out,
        bias_out_sum,
        ln2_gain_sum,
        ln2_shift_sum,
        sum_up,
        vectors[:ff],
        sum_down,
        bias_down_sum,
    )


def solution(mesh):
    split = P("row", "seq", None)
    placed = (split, P("row", None)) + (P(),) * 13 + (split,)
    return jax.shard_map(
        functools.partial(per_device, mesh.shape["seq"], mesh.shape["row"]),
        mesh=mesh,
        in_specs=placed,
        out_specs=(split, split) + (P(),) * 13,
        check_vma=False,
    )
```

profile of v0, /device:TPU:0, one launch (start us, length us, event | category | flops | bytes accessed | tf_op | source)
XLA Modules:
  0.0 134.5 jit_solution(17422097465049746283)
XLA Ops:
  1.9 4.0 %collective-permute-start.2 = (bf16[128,512]{1,0:T(8,128)(2,1)S(1)}, bf16[128,512]{1,0:T(8,128)(2,1)S(1)}, u32[]{:S(2)}, u32[]{:S(2)}) collective-permute-start(bf16[128,512]{1,0:T(8,128)(2,1)S(1)} %get-tuple-element.317), channel_id=1, source_target_pairs={{0,24},{4,28},{8,16},{12,20},{16,8},{20,12},{24,0},{28,4},{1,25},{... | collective-permute-start | bytes 393224 | tf_op jit(solution)/shard_map/ppermute | solution.py:766
  8.2 1.9 %collective-permute-done.2.refs_3_ = bf16[128,512]{1,0:T(8,128)(2,1)S(1)} collective-permute-done((bf16[128,512]{1,0:T(8,128)(2,1)S(1)}, bf16[128,512]{1,0:T(8,128)(2,1)S(1)}, u32[]{:S(2)}, u32[]{:S(2)}) %collective-permute-start.2) | collective-permute-done | bytes 131104 | tf_op jit(solution)/shard_map/ppermute | solution.py:766
  10.1 2.2 %collective-permute-done.refs_1_ = bf16[128,512]{1,0:T(8,128)(2,1)S(1)} collective-permute-done((bf16[128,512]{1,0:T(8,128)(2,1)S(1)}, bf16[128,512]{1,0:T(8,128)(2,1)S(1)}, u32[]{:S(2)}, u32[]{:S(2)}) %collective-permute-start) | collective-permute-done | bytes 131104 | tf_op jit(solution)/shard_map/ppermute | solution.py:766
  17.6 1.6 %collective-permute-start.3 = (bf16[128,512]{1,0:T(8,128)(2,1)S(1)}, bf16[128,512]{1,0:T(8,128)(2,1)S(1)}, u32[]{:S(2)}, u32[]{:S(2)}) collective-permute-start(bf16[128,512]{1,0:T(8,128)(2,1)S(1)} %get-tuple-element.162), channel_id=1, source_target_pairs={{0,8},{4,12},{8,0},{12,4},{16,24},{20,28},{24,16},{28,20},{1,9},{5... | collective-permute-start | bytes 393224 | tf_op jit(solution)/shard_map/ppermute | solution.py:766
  21.3 7.0 %attention_forward.1 = (f32[512,512]{1,0:T(8,128)S(1)}, bf16[512,512]{1,0:T(8,128)(2,1)S(1)}) custom-call(bf16[512,512]{1,0:T(8,128)(2,1)S(1)} %get-tuple-element.166.refs_0_, bf16[512,1024]{1,0:T(8,128)(2,1)S(1)} %get-tuple-element.160.refs_1_.refs_3_.refs_4_.refs_6_, bf16[512,1024]{1,0:T(8,128)(2,1)S(1)} %collective-permute-done.6.refs_2_.refs_4_.refs_5_.refs_7_, ...), custom_call_target="tpu_custom_call" | custom-call | flops 1073741824 | bytes 2097152 | tf_op jit(solution)/shard_map/attention_forward/pallas_call | solution.py:177
  28.4 8.2 %middle_part.1 = (bf16[128,512]{1,0:T(8,128)(2,1)S(1)}, bf16[128,512]{1,0:T(8,128)(2,1)S(1)}, bf16[128,512]{1,0:T(8,128)(2,1)S(1)}, bf16[128,512]{1,0:T(8,128)(2...) custom-call(bf16[128,512]{1,0:T(8,128)(2,1)S(1)} %get-tuple-element., ...), custom_call_target="tpu_custom_call" | custom-call | flops 5637144576 | bytes 8388608 | tf_op jit(solution)/shard_map/middle_part/pallas_call | solution.py:354
  36.6 2.6 %grad_up_out.1 = (bf16[256,2560]{1,0:T(8,128)(2,1)S(1)}, bf16[256,2560]{1,0:T(8,128)(2,1)S(1)}) custom-call(s32[4]{0:T(128)S(1)} %pad_add_fusion.marks.refs_0_, bf16[512,512]{1,0:T(8,128)(2,1)S(1)} %get-tuple-element.175.refs_0_, bf16[512,2048]{1,0:T(8,128)(2,1)S(1)} %get-tuple-element.176.refs_1_, bf16[512,512]{1,0:T(8,128)(2,1)S(1)} %get-tuple-element.177.refs_2_, ...), custom_call_target="tpu_custom_call" | custom-call | flops 1342177280 | bytes 7864320 | tf_op jit(solution)/shard_map/grad_up_out/pallas_call | solution.py:427
  39.3 2.6 %grad_down.1 = (bf16[1024,512]{1,0:T(8,128)(2,1)S(1)}, bf16[1024,512]{1,0:T(8,128)(2,1)S(1)}) custom-call(s32[4]{0:T(128)S(1)} %pad_add_fusion.marks.refs_0_, bf16[512,2048]{1,0:T(8,128)(2,1)S(1)} %get-tuple-element.180.refs_0_, bf16[512,512]{1,0:T(8,128)(2,1)S(1)} %get-tuple-element.181.refs_1_), custom_call_target="tpu_custom_call" | custom-call | flops 1073741824 | bytes 6291456 | tf_op jit(solution)/shard_map/grad_down/pallas_call | solution.py:427
  42.9 1.5 %collective-permute-start.10 = (bf16[128,1280]{1,0:T(8,128)(2,1)S(1)}, bf16[128,1280]{1,0:T(8,128)(2,1)S(1)}, u32[]{:S(2)}, u32[]{:S(2)}) collective-permute-start(bf16[128,1280]{1,0:T(8,128)(2,1)S(1)} %get-tuple-element.305), channel_id=1, source_target_pairs={{0,16},{4,20},{8,24},{12,28},{16,0},{20,4},{24,8},{28,12},{1,17},{... | collective-permute-start | bytes 983048 | tf_op jit(solution)/shard_map/ppermute | solution.py:589
  45.9 5.4 %attention_backward.2 = (bf16[512,256]{1,0:T(8,128)(2,1)S(1)}, f32[512,512]{1,0:T(8,128)S(1)}, bf16[512,512]{1,0:T(8,128)(2,1)S(1)}) custom-call(bf16[512,512]{1,0:T(8,128)(2,1)S(1)} %get-tuple-element.166.refs_0_, bf16[512,512]{1,0:T(8,128)(2,1)S(1)} %get-tuple-element.198.refs_1_, bf16[512,512]{1,0:T(8,128)(2,1)S(1)} %get-tuple-element.189.refs_2_, ...), custom_call_target="tpu_custom_call" | custom-call | flops 1342177280 | bytes 1572864 | tf_op jit(solution)/shard_map/attention_backward/pallas_call | solution.py:258
  54.7 1.5 %collective-permute-start.12 = (bf16[64,1280]{1,0:T(8,128)(2,1)S(1)}, bf16[64,1280]{1,0:T(8,128)(2,1)S(1)}, u32[]{:S(2)}, u32[]{:S(2)}) collective-permute-start(bf16[64,1280]{1,0:T(8,128)(2,1)S(1)} %get-tuple-element.337), channel_id=1, source_target_pairs={{0,8},{4,12},{8,0},{12,4},{16,24},{20,28},{24,16},{28,20},{1,9},{5... | collective-permute-start | bytes 491528 | tf_op jit(solution)/shard_map/ppermute | solution.py:589
  56.3 5.4 %attention_backward.3 = (bf16[512,256]{1,0:T(8,128)(2,1)S(1)}, f32[512,512]{1,0:T(8,128)S(1)}, bf16[512,512]{1,0:T(8,128)(2,1)S(1)}) custom-call(bf16[512,512]{1,0:T(8,128)(2,1)S(1)} %get-tuple-element.166.refs_0_, bf16[512,512]{1,0:T(8,128)(2,1)S(1)} %get-tuple-element.198.refs_1_, bf16[512,512]{1,0:T(8,128)(2,1)S(1)} %get-tuple-element.189.refs_2_, ...), custom_call_target="tpu_custom_call" | custom-call | flops 1342177280 | bytes 1572864 | tf_op jit(solution)/shard_map/attention_backward/pallas_call | solution.py:258
  62.4 1.6 %collective-permute-start.18 = (bf16[32,2560]{1,0:T(8,128)(2,1)S(1)}, bf16[32,2560]{1,0:T(8,128)(2,1)S(1)}, u32[]{:S(2)}, u32[]{:S(2)}) collective-permute-start(bf16[32,2560]{1,0:T(8,128)(2,1)S(1)} %pad_maximum_fusion.2), channel_id=1, source_target_pairs={{0,1},{1,0},{2,3},{3,2},{4,5},{5,4},{6,7},{7,6},{8,9},{9,8},{10,11... | collective-permute-start | bytes 491528 | tf_op jit(solution)/shard_map/ppermute | solution.py:589
  65.1 1.5 %collective-permute-start.14 = (bf16[512,384]{1,0:T(8,128)(2,1)S(1)}, bf16[512,384]{1,0:T(8,128)(2,1)S(1)}, u32[]{:S(2)}, u32[]{:S(2)}) collective-permute-start(bf16[512,384]{1,0:T(8,128)(2,1)S(1)} %fusion.19), channel_id=1, source_target_pairs={{0,16},{4,20},{8,24},{12,28},{16,0},{20,4},{24,8},{28,12},{1,17},{... | collective-permute-start | bytes 1179656 | tf_op jit(solution)/shard_map/ppermute | solution.py:589
  66.6 3.0 %qkv_grad.1 = (bf16[512,1536]{1,0:T(8,128)(2,1)S(1)}, bf16[256,1664]{1,0:T(8,128)(2,1)S(1)}, bf16[256,1664]{1,0:T(8,128)(2,1)S(1)}) custom-call(s32[4]{0:T(128)S(1)} %pad_add_fusion.marks.refs_0_, bf16[512,512]{1,0:T(8,128)(2,1)S(1)} %copy-done.5, f32[12,512]{1,0:T(8,128)S(1)} %concatenate.140.refs_4_.refs_6_.refs_2_.small, bf16[512,1536]{1,0:T(8,128)(2,1)S(1)} %copy-done.3, ...), custom_call_target="tpu_custom_call" | custom-call | flops 805306368 | bytes 4718592 | tf_op jit(solution)/shard_map/qkv_grad/pallas_call | solution.py:481
  69.8 2.7 %collective-permute-start.23 = (bf16[32,2560]{1,0:T(8,128)(2,1)S(1)}, bf16[32,2560]{1,0:T(8,128)(2,1)S(1)}, u32[]{:S(2)}, u32[]{:S(2)}) collective-permute-start(bf16[32,2560]{1,0:T(8,128)(2,1)S(1)} %add_convert_fusion.10), channel_id=1, source_target_pairs={{0,2},{1,3},{2,0},{3,1},{4,6},{5,7},{6,4},{7,5},{8,10},{9,11},{10,... | collective-permute-start | bytes 491528 | tf_op jit(solution)/shard_map/ppermute | solution.py:589
  72.7 1.6 %collective-permute-start.21 = (bf16[128,768]{1,0:T(8,128)(2,1)S(1)}, bf16[128,768]{1,0:T(8,128)(2,1)S(1)}, u32[]{:S(2)}, u32[]{:S(2)}) collective-permute-start(bf16[128,768]{1,0:T(8,128)(2,1)S(1)} %get-tuple-element.316), channel_id=1, source_target_pairs={{0,8},{4,12},{8,0},{12,4},{16,24},{20,28},{24,16},{28,20},{1,9},{5... | collective-permute-start | bytes 589832 | tf_op jit(solution)/shard_map/ppermute | solution.py:589
  76.0 1.5 %collective-permute-start.20 = (bf16[256,512]{1,0:T(8,128)(2,1)S(1)}, bf16[256,512]{1,0:T(8,128)(2,1)S(1)}, u32[]{:S(2)}, u32[]{:S(2)}) collective-permute-start(bf16[256,512]{1,0:T(8,128)(2,1)S(1)} %maximum_maximum_fusion.5), channel_id=1, source_target_pairs={{0,8},{4,12},{8,0},{12,4},{16,24},{20,28},{24,16},{28,20},{1,9},{5... | collective-permute-start | bytes 786440 | tf_op jit(solution)/shard_map/ppermute | solution.py:589
  77.5 2.0 %collective-permute-start.19 = (bf16[256,512]{1,0:T(8,128)(2,1)S(1)}, bf16[256,512]{1,0:T(8,128)(2,1)S(1)}, u32[]{:S(2)}, u32[]{:S(2)}) collective-permute-start(bf16[256,512]{1,0:T(8,128)(2,1)S(1)} %fusion.22), channel_id=1, source_target_pairs={{0,16},{4,20},{8,24},{12,28},{16,0},{20,4},{24,8},{28,12},{1,17},{... | collective-permute-start | bytes 786440 | tf_op jit(solution)/shard_map/ppermute | solution.py:589
  85.4 3.1 %collective-permute-done.19 = bf16[256,512]{1,0:T(8,128)(2,1)S(1)} collective-permute-done((bf16[256,512]{1,0:T(8,128)(2,1)S(1)}, bf16[256,512]{1,0:T(8,128)(2,1)S(1)}, u32[]{:S(2)}, u32[]{:S(2)}) %collective-permute-start.19) | collective-permute-done | bytes 262176 | tf_op jit(solution)/shard_map/ppermute | solution.py:589
  92.4 1.7 %collective-permute-done.24 = bf16[128,512]{1,0:T(8,128)(2,1)S(1)} collective-permute-done((bf16[128,512]{1,0:T(8,128)(2,1)S(1)}, bf16[128,512]{1,0:T(8,128)(2,1)S(1)}, u32[]{:S(2)}, u32[]{:S(2)}) %collective-permute-start.24) | collective-permute-done | bytes 131104 | tf_op jit(solution)/shard_map/ppermute | solution.py:589
  94.1 3.2 %collective-permute-start.28 = (bf16[128,512]{1,0:T(8,128)(2,1)S(1)}, bf16[128,512]{1,0:T(8,128)(2,1)S(1)}, u32[]{:S(2)}, u32[]{:S(2)}) collective-permute-start(bf16[128,512]{1,0:T(8,128)(2,1)S(1)} %add_convert_fusion.14), channel_id=1, source_target_pairs={{0,2},{1,3},{2,0},{3,1},{4,6},{5,7},{6,4},{7,5},{8,10},{9,11},{10,... | collective-permute-start | bytes 393224 | tf_op jit(solution)/shard_map/ppermute | solution.py:589
  97.3 1.7 %collective-permute-start.35 = (bf16[32,1664]{1,0:T(8,128)(2,1)S(1)}, bf16[32,1664]{1,0:T(8,128)(2,1)S(1)}, u32[]{:S(2)}, u32[]{:S(2)}) collective-permute-start(bf16[32,1664]{1,0:T(8,128)(2,1)S(1)} %add_convert_fusion.19), channel_id=1, source_target_pairs={{0,2},{1,3},{2,0},{3,1},{4,6},{5,7},{6,4},{7,5},{8,10},{9,11},{10,... | collective-permute-start | bytes 319496 | tf_op jit(solution)/shard_map/ppermute | solution.py:589
  99.8 1.6 %collective-permute-start.33 = (bf16[128,1792]{1,0:T(8,128)(2,1)S(1)}, bf16[128,1792]{1,0:T(8,128)(2,1)S(1)}, u32[]{:S(2)}, u32[]{:S(2)}) collective-permute-start(bf16[128,1792]{1,0:T(8,128)(2,1)S(1)} %maximum_maximum_fusion.4), channel_id=1, source_target_pairs={{0,16},{4,20},{8,24},{12,28},{16,0},{20,4},{24,8},{28,12},{1,17},{... | collective-permute-start | bytes 1376264 | tf_op jit(solution)/shard_map/ppermute | solution.py:589
  101.3 1.8 %collective-permute-done.28 = bf16[128,512]{1,0:T(8,128)(2,1)S(1)} collective-permute-done((bf16[128,512]{1,0:T(8,128)(2,1)S(1)}, bf16[128,512]{1,0:T(8,128)(2,1)S(1)}, u32[]{:S(2)}, u32[]{:S(2)}) %collective-permute-start.28) | collective-permute-done | bytes 131104 | tf_op jit(solution)/shard_map/ppermute | solution.py:589
  106.3 2.0 %collective-permute-done.34 = bf16[128,512]{1,0:T(8,128)(2,1)S(1)} collective-permute-done((bf16[128,512]{1,0:T(8,128)(2,1)S(1)}, bf16[128,512]{1,0:T(8,128)(2,1)S(1)}, u32[]{:S(2)}, u32[]{:S(2)}) %collective-permute-start.34) | collective-permute-done | bytes 131104 | tf_op jit(solution)/shard_map/ppermute | solution.py:589
  113.7 1.9 %collective-permute-start.44 = (bf16[512,256]{1,0:T(8,128)(2,1)S(1)}, bf16[512,256]{1,0:T(8,128)(2,1)S(1)}, u32[]{:S(2)}, u32[]{:S(2)}) collective-permute-start(bf16[512,256]{1,0:T(8,128)(2,1)S(1)} %constant_dynamic-update-slice_fusion.19), channel_id=1, source_target_pairs={{0,16},{4,20},{8,24},{12,28},{16,0},{20,4},{24,8},{28,12},{1,17},{... | collective-permute-start | bytes 786440 | tf_op jit(solution)/shard_map/ppermute | solution.py:589
  116.8 2.2 %collective-permute-start.41 = (bf16[128,768]{1,0:T(8,128)(2,1)S(1)}, bf16[128,768]{1,0:T(8,128)(2,1)S(1)}, u32[]{:S(2)}, u32[]{:S(2)}) collective-permute-start(bf16[128,768]{1,0:T(8,128)(2,1)S(1)} %constant_dynamic-update-slice_fusion.21), channel_id=1, source_target_pairs={{0,8},{4,12},{8,0},{12,4},{16,24},{20,28},{24,16},{28,20},{1,9},{5... | collective-permute-start | bytes 589832 | tf_op jit(solution)/shard_map/ppermute | solution.py:589
  121.3 3.4 %assemble_up_out.1 = (f32[512,2048]{1,0:T(8,128)}, f32[512,512]{1,0:T(8,128)}) custom-call(s32[4]{0:T(128)S(1)} %pad_add_fusion.marks.refs_0_, bf16[256,2560]{1,0:T(8,128)(2,1)S(1)} %maximum_maximum_fusion.refs_0_, bf16[256,2560]{1,0:T(8,128)(2,1)S(1)} %collective-permute-done.45.refs_1_), custom_call_target="tpu_custom_call" | custom-call | flops 1310720 | bytes 7864320 | tf_op jit(solution)/shard_map/assemble_up_out/pallas_call | solution.py:548
  124.8 1.8 %collective-permute-done.41 = bf16[128,768]{1,0:T(8,128)(2,1)S(1)} collective-permute-done((bf16[128,768]{1,0:T(8,128)(2,1)S(1)}, bf16[128,768]{1,0:T(8,128)(2,1)S(1)}, u32[]{:S(2)}, u32[]{:S(2)}) %collective-permute-start.41) | collective-permute-done | bytes 196640 | tf_op jit(solution)/shard_map/ppermute | solution.py:589
  127.5 3.0 %assemble_down.1 = f32[2048,512]{1,0:T(8,128)} custom-call(s32[4]{0:T(128)S(1)} %pad_add_fusion.marks.refs_0_, bf16[1024,512]{1,0:T(8,128)(2,1)S(1)} %maximum_maximum_fusion.1.refs_0_, bf16[1024,512]{1,0:T(8,128)(2,1)S(1)} %collective-permute-done.47.refs_1_), custom_call_target="tpu_custom_call" | custom-call | flops 1048576 | bytes 6291456 | tf_op jit(solution)/shard_map/assemble_down/pallas_call | solution.py:548
  130.5 2.6 %assemble_qkv.1 = (f32[512,1536]{1,0:T(8,128)}, f32[512,128]{1,0:T(8,128)S(1)}) custom-call(s32[4]{0:T(128)S(1)} %pad_add_fusion.marks.refs_0_, bf16[256,1664]{1,0:T(8,128)(2,1)S(1)} %maximum_maximum_fusion.2.refs_0_, bf16[256,1664]{1,0:T(8,128)(2,1)S(1)} %collective-permute-done.46.refs_1_), custom_call_target="tpu_custom_call" | custom-call | flops 851968 | bytes 5111808 | tf_op jit(solution)/shard_map/assemble_qkv/pallas_call | solution.py:548
  (221 shorter events, 44.9 us)
Async XLA Ops:
  1.9 8.3 %collective-permute-start.2 = (bf16[128,512]{1,0:T(8,128)(2,1)S(1)}, bf16[128,512]{1,0:T(8,128)(2,1)S(1)}, u32[]{:S(2)}, u32[]{:S(2)}) collective-permute-start(bf16[128,512]{1,0:T(8,128)(2,1)S(1)} %get-tuple-element.317), channel_id=1, source_target_pairs={{0,24},{4,28},{8,16},{12,20},{16,8},{20,12},{24,0},{28,4},{1,25},{... | collective-permute-start | bytes 393224 | tf_op jit(solution)/shard_map/ppermute | solution.py:766
  17.6 10.7 %collective-permute-start.3 = (bf16[128,512]{1,0:T(8,128)(2,1)S(1)}, bf16[128,512]{1,0:T(8,128)(2,1)S(1)}, u32[]{:S(2)}, u32[]{:S(2)}) collective-permute-start(bf16[128,512]{1,0:T(8,128)(2,1)S(1)} %get-tuple-element.162), channel_id=1, source_target_pairs={{0,8},{4,12},{8,0},{12,4},{16,24},{20,28},{24,16},{28,20},{1,9},{5... | collective-permute-start | bytes 393224 | tf_op jit(solution)/shard_map/ppermute | solution.py:766
  19.2 9.1 %collective-permute-start.4 = (bf16[128,512]{1,0:T(8,128)(2,1)S(1)}, bf16[128,512]{1,0:T(8,128)(2,1)S(1)}, u32[]{:S(2)}, u32[]{:S(2)}) collective-permute-start(bf16[128,512]{1,0:T(8,128)(2,1)S(1)} %get-tuple-element.163), channel_id=1, source_target_pairs={{0,16},{4,20},{8,24},{12,28},{16,0},{20,4},{24,8},{28,12},{1,17},{... | collective-permute-start | bytes 393224 | tf_op jit(solution)/shard_map/ppermute | solution.py:766
  20.6 7.7 %collective-permute-start.5 = (bf16[128,512]{1,0:T(8,128)(2,1)S(1)}, bf16[128,512]{1,0:T(8,128)(2,1)S(1)}, u32[]{:S(2)}, u32[]{:S(2)}) collective-permute-start(bf16[128,512]{1,0:T(8,128)(2,1)S(1)} %get-tuple-element.164), channel_id=1, source_target_pairs={{0,24},{4,28},{8,16},{12,20},{16,8},{20,12},{24,0},{28,4},{1,25},{... | collective-permute-start | bytes 393224 | tf_op jit(solution)/shard_map/ppermute | solution.py:766
  41.9 22.1 %collective-permute-start.7 = (bf16[1024,512]{1,0:T(8,128)(2,1)S(1)}, bf16[1024,512]{1,0:T(8,128)(2,1)S(1)}, u32[]{:S(2)}, u32[]{:S(2)}) collective-permute-start(bf16[1024,512]{1,0:T(8,128)(2,1)S(1)} %get-tuple-element.183), channel_id=1, source_target_pairs={{0,4},{4,0},{8,12},{12,8},{16,20},{20,16},{24,28},{28,24},{1,5},{5... | collective-permute-start | bytes 3145736 | tf_op jit(solution)/shard_map/ppermute | solution.py:589
  42.9 9.7 %collective-permute-start.10 = (bf16[128,1280]{1,0:T(8,128)(2,1)S(1)}, bf16[128,1280]{1,0:T(8,128)(2,1)S(1)}, u32[]{:S(2)}, u32[]{:S(2)}) collective-permute-start(bf16[128,1280]{1,0:T(8,128)(2,1)S(1)} %get-tuple-element.305), channel_id=1, source_target_pairs={{0,16},{4,20},{8,24},{12,28},{16,0},{20,4},{24,8},{28,12},{1,17},{... | collective-permute-start | bytes 983048 | tf_op jit(solution)/shard_map/ppermute | solution.py:589
  44.4 9.4 %collective-permute-start.9 = (bf16[128,1280]{1,0:T(8,128)(2,1)S(1)}, bf16[128,1280]{1,0:T(8,128)(2,1)S(1)}, u32[]{:S(2)}, u32[]{:S(2)}) collective-permute-start(bf16[128,1280]{1,0:T(8,128)(2,1)S(1)} %get-tuple-element.306), channel_id=1, source_target_pairs={{0,8},{4,12},{8,0},{12,4},{16,24},{20,28},{24,16},{28,20},{1,9},{5... | collective-permute-start | bytes 983048 | tf_op jit(solution)/shard_map/ppermute | solution.py:589
  53.9 8.3 %collective-permute-start.11 = (bf16[64,1280]{1,0:T(8,128)(2,1)S(1)}, bf16[64,1280]{1,0:T(8,128)(2,1)S(1)}, u32[]{:S(2)}, u32[]{:S(2)}) collective-permute-start(bf16[64,1280]{1,0:T(8,128)(2,1)S(1)} %get-tuple-element.339), channel_id=1, source_target_pairs={{0,16},{4,20},{8,24},{12,28},{16,0},{20,4},{24,8},{28,12},{1,17},{... | collective-permute-start | bytes 491528 | tf_op jit(solution)/shard_map/ppermute | solution.py:589
  54.7 7.5 %collective-permute-start.12 = (bf16[64,1280]{1,0:T(8,128)(2,1)S(1)}, bf16[64,1280]{1,0:T(8,128)(2,1)S(1)}, u32[]{:S(2)}, u32[]{:S(2)}) collective-permute-start(bf16[64,1280]{1,0:T(8,128)(2,1)S(1)} %get-tuple-element.337), channel_id=1, source_target_pairs={{0,8},{4,12},{8,0},{12,4},{16,24},{20,28},{24,16},{28,20},{1,9},{5... | collective-permute-start | bytes 491528 | tf_op jit(solution)/shard_map/ppermute | solution.py:589
  56.2 10.4 %collective-permute-start.15 = (bf16[512,512]{1,0:T(8,128)(2,1)S(1)}, bf16[512,512]{1,0:T(8,128)(2,1)S(1)}, u32[]{:S(2)}, u32[]{:S(2)}) collective-permute-start(bf16[512,512]{1,0:T(8,128)(2,1)S(1)} %get-tuple-element.193), channel_id=1, source_target_pairs={{0,4},{4,0},{8,12},{12,8},{16,20},{20,16},{24,28},{28,24},{1,5},{5... | collective-permute-start | bytes 1572872 | tf_op jit(solution)/shard_map/ppermute | solution.py:589
  62.4 7.4 %collective-permute-start.18 = (bf16[32,2560]{1,0:T(8,128)(2,1)S(1)}, bf16[32,2560]{1,0:T(8,128)(2,1)S(1)}, u32[]{:S(2)}, u32[]{:S(2)}) collective-permute-start(bf16[32,2560]{1,0:T(8,128)(2,1)S(1)} %pad_maximum_fusion.2), channel_id=1, source_target_pairs={{0,1},{1,0},{2,3},{3,2},{4,5},{5,4},{6,7},{7,6},{8,9},{9,8},{10,11... | collective-permute-start | bytes 491528 | tf_op jit(solution)/shard_map/ppermute | solution.py:589
  64.4 10.8 %collective-permute-start.13 = (bf16[512,384]{1,0:T(8,128)(2,1)S(1)}, bf16[512,384]{1,0:T(8,128)(2,1)S(1)}, u32[]{:S(2)}, u32[]{:S(2)}) collective-permute-start(bf16[512,384]{1,0:T(8,128)(2,1)S(1)} %fusion.13), channel_id=1, source_target_pairs={{0,8},{4,12},{8,0},{12,4},{16,24},{20,28},{24,16},{28,20},{1,9},{5... | collective-permute-start | bytes 1179656 | tf_op jit(solution)/shard_map/ppermute | solution.py:589
  65.1 10.6 %collective-permute-start.14 = (bf16[512,384]{1,0:T(8,128)(2,1)S(1)}, bf16[512,384]{1,0:T(8,128)(2,1)S(1)}, u32[]{:S(2)}, u32[]{:S(2)}) collective-permute-start(bf16[512,384]{1,0:T(8,128)(2,1)S(1)} %fusion.19), channel_id=1, source_target_pairs={{0,16},{4,20},{8,24},{12,28},{16,0},{20,4},{24,8},{28,12},{1,17},{... | collective-permute-start | bytes 1179656 | tf_op jit(solution)/shard_map/ppermute | solution.py:589
  69.8 11.0 %collective-permute-start.23 = (bf16[32,2560]{1,0:T(8,128)(2,1)S(1)}, bf16[32,2560]{1,0:T(8,128)(2,1)S(1)}, u32[]{:S(2)}, u32[]{:S(2)}) collective-permute-start(bf16[32,2560]{1,0:T(8,128)(2,1)S(1)} %add_convert_fusion.10), channel_id=1, source_target_pairs={{0,2},{1,3},{2,0},{3,1},{4,6},{5,7},{6,4},{7,5},{8,10},{9,11},{10,... | collective-permute-start | bytes 491528 | tf_op jit(solution)/shard_map/ppermute | solution.py:589
  72.7 9.5 %collective-permute-start.21 = (bf16[128,768]{1,0:T(8,128)(2,1)S(1)}, bf16[128,768]{1,0:T(8,128)(2,1)S(1)}, u32[]{:S(2)}, u32[]{:S(2)}) collective-permute-start(bf16[128,768]{1,0:T(8,128)(2,1)S(1)} %get-tuple-element.316), channel_id=1, source_target_pairs={{0,8},{4,12},{8,0},{12,4},{16,24},{20,28},{24,16},{28,20},{1,9},{5... | collective-permute-start | bytes 589832 | tf_op jit(solution)/shard_map/ppermute | solution.py:589
  74.3 8.5 %collective-permute-start.22 = (bf16[128,896]{1,0:T(8,128)(2,1)S(1)}, bf16[128,896]{1,0:T(8,128)(2,1)S(1)}, u32[]{:S(2)}, u32[]{:S(2)}) collective-permute-start(bf16[128,896]{1,0:T(8,128)(2,1)S(1)} %get-tuple-element.314), channel_id=1, source_target_pairs={{0,16},{4,20},{8,24},{12,28},{16,0},{20,4},{24,8},{28,12},{1,17},{... | collective-permute-start | bytes 688136 | tf_op jit(solution)/shard_map/ppermute | solution.py:589
  76.0 9.5 %collective-permute-start.20 = (bf16[256,512]{1,0:T(8,128)(2,1)S(1)}, bf16[256,512]{1,0:T(8,128)(2,1)S(1)}, u32[]{:S(2)}, u32[]{:S(2)}) collective-permute-start(bf16[256,512]{1,0:T(8,128)(2,1)S(1)} %maximum_maximum_fusion.5), channel_id=1, source_target_pairs={{0,8},{4,12},{8,0},{12,4},{16,24},{20,28},{24,16},{28,20},{1,9},{5... | collective-permute-start | bytes 786440 | tf_op jit(solution)/shard_map/ppermute | solution.py:589
  77.5 11.0 %collective-permute-start.19 = (bf16[256,512]{1,0:T(8,128)(2,1)S(1)}, bf16[256,512]{1,0:T(8,128)(2,1)S(1)}, u32[]{:S(2)}, u32[]{:S(2)}) collective-permute-start(bf16[256,512]{1,0:T(8,128)(2,1)S(1)} %fusion.22), channel_id=1, source_target_pairs={{0,16},{4,20},{8,24},{12,28},{16,0},{20,4},{24,8},{28,12},{1,17},{... | collective-permute-start | bytes 786440 | tf_op jit(solution)/shard_map/ppermute | solution.py:589
  80.8 8.4 %collective-permute-start.27 = (bf16[32,2560]{1,0:T(8,128)(2,1)S(1)}, bf16[32,2560]{1,0:T(8,128)(2,1)S(1)}, u32[]{:S(2)}, u32[]{:S(2)}) collective-permute-start(bf16[32,2560]{1,0:T(8,128)(2,1)S(1)} %add_convert_fusion.9), channel_id=1, source_target_pairs={{0,1},{1,0},{2,3},{3,2},{4,5},{5,4},{6,7},{7,6},{8,9},{9,8},{10,11... | collective-permute-start | bytes 491528 | tf_op jit(solution)/shard_map/ppermute | solution.py:589
  82.9 7.8 %collective-permute-start.25 = (bf16[64,768]{1,0:T(8,128)(2,1)S(1)}, bf16[64,768]{1,0:T(8,128)(2,1)S(1)}, u32[]{:S(2)}, u32[]{:S(2)}) collective-permute-start(bf16[64,768]{1,0:T(8,128)(2,1)S(1)} %get-tuple-element.362), channel_id=1, source_target_pairs={{0,16},{4,20},{8,24},{12,28},{16,0},{20,4},{24,8},{28,12},{1,17},{... | collective-permute-start | bytes 294920 | tf_op jit(solution)/shard_map/ppermute | solution.py:589
  83.7 7.1 %collective-permute-start.26 = (bf16[64,896]{1,0:T(8,128)(2,1)S(1)}, bf16[64,896]{1,0:T(8,128)(2,1)S(1)}, u32[]{:S(2)}, u32[]{:S(2)}) collective-permute-start(bf16[64,896]{1,0:T(8,128)(2,1)S(1)} %get-tuple-element.360), channel_id=1, source_target_pairs={{0,8},{4,12},{8,0},{12,4},{16,24},{20,28},{24,16},{28,20},{1,9},{5... | collective-permute-start | bytes 344072 | tf_op jit(solution)/shard_map/ppermute | solution.py:589
  89.4 9.7 %collective-permute-start.30 = (bf16[64,2304]{1,0:T(8,128)(2,1)S(1)}, bf16[64,2304]{1,0:T(8,128)(2,1)S(1)}, u32[]{:S(2)}, u32[]{:S(2)}) collective-permute-start(bf16[64,2304]{1,0:T(8,128)(2,1)S(1)} %get-tuple-element.369), channel_id=1, source_target_pairs={{0,8},{4,12},{8,0},{12,4},{16,24},{20,28},{24,16},{28,20},{1,9},{5... | collective-permute-start | bytes 884744 | tf_op jit(solution)/shard_map/ppermute | solution.py:589
  89.5 9.5 %collective-permute-start.29 = (bf16[64,2304]{1,0:T(8,128)(2,1)S(1)}, bf16[64,2304]{1,0:T(8,128)(2,1)S(1)}, u32[]{:S(2)}, u32[]{:S(2)}) collective-permute-start(bf16[64,2304]{1,0:T(8,128)(2,1)S(1)} %get-tuple-element.370), channel_id=1, source_target_pairs={{0,16},{4,20},{8,24},{12,28},{16,0},{20,4},{24,8},{28,12},{1,17},{... | collective-permute-start | bytes 884744 | tf_op jit(solution)/shard_map/ppermute | solution.py:589
  94.1 9.1 %collective-permute-start.28 = (bf16[128,512]{1,0:T(8,128)(2,1)S(1)}, bf16[128,512]{1,0:T(8,128)(2,1)S(1)}, u32[]{:S(2)}, u32[]{:S(2)}) collective-permute-start(bf16[128,512]{1,0:T(8,128)(2,1)S(1)} %add_convert_fusion.14), channel_id=1, source_target_pairs={{0,2},{1,3},{2,0},{3,1},{4,6},{5,7},{6,4},{7,5},{8,10},{9,11},{10,... | collective-permute-start | bytes 393224 | tf_op jit(solution)/shard_map/ppermute | solution.py:589
  97.3 7.8 %collective-permute-start.35 = (bf16[32,1664]{1,0:T(8,128)(2,1)S(1)}, bf16[32,1664]{1,0:T(8,128)(2,1)S(1)}, u32[]{:S(2)}, u32[]{:S(2)}) collective-permute-start(bf16[32,1664]{1,0:T(8,128)(2,1)S(1)} %add_convert_fusion.19), channel_id=1, source_target_pairs={{0,2},{1,3},{2,0},{3,1},{4,6},{5,7},{6,4},{7,5},{8,10},{9,11},{10,... | collective-permute-start | bytes 319496 | tf_op jit(solution)/shard_map/ppermute | solution.py:589
  99.2 10.9 %collective-permute-start.32 = (bf16[128,1792]{1,0:T(8,128)(2,1)S(1)}, bf16[128,1792]{1,0:T(8,128)(2,1)S(1)}, u32[]{:S(2)}, u32[]{:S(2)}) collective-permute-start(bf16[128,1792]{1,0:T(8,128)(2,1)S(1)} %maximum_maximum_fusion.3), channel_id=1, source_target_pairs={{0,8},{4,12},{8,0},{12,4},{16,24},{20,28},{24,16},{28,20},{1,9},{5... | collective-permute-start | bytes 1376264 | tf_op jit(solution)/shard_map/ppermute | solution.py:589
  99.8 10.7 %collective-permute-start.33 = (bf16[128,1792]{1,0:T(8,128)(2,1)S(1)}, bf16[128,1792]{1,0:T(8,128)(2,1)S(1)}, u32[]{:S(2)}, u32[]{:S(2)}) collective-permute-start(bf16[128,1792]{1,0:T(8,128)(2,1)S(1)} %maximum_maximum_fusion.4), channel_id=1, source_target_pairs={{0,16},{4,20},{8,24},{12,28},{16,0},{20,4},{24,8},{28,12},{1,17},{... | collective-permute-start | bytes 1376264 | tf_op jit(solution)/shard_map/ppermute | solution.py:589
  110.7 10.6 %collective-permute-start.45 = (bf16[256,2560]{1,0:T(8,128)(2,1)S(1)}, bf16[256,2560]{1,0:T(8,128)(2,1)S(1)}, u32[]{:S(2)}, u32[]{:S(2)}) collective-permute-start(bf16[256,2560]{1,0:T(8,128)(2,1)S(1)} %maximum_maximum_fusion.refs_0_), channel_id=1, source_target_pairs={{0,4},{4,0},{8,12},{12,8},{16,20},{20,16},{24,28},{28,24},{1,5},{5... | collective-permute-start | bytes 3932168 | tf_op jit(solution)/shard_map/ppermute | solution.py:589
  113.7 10.9 %collective-permute-start.44 = (bf16[512,256]{1,0:T(8,128)(2,1)S(1)}, bf16[512,256]{1,0:T(8,128)(2,1)S(1)}, u32[]{:S(2)}, u32[]{:S(2)}) collective-permute-start(bf16[512,256]{1,0:T(8,128)(2,1)S(1)} %constant_dynamic-update-slice_fusion.19), channel_id=1, source_target_pairs={{0,16},{4,20},{8,24},{12,28},{16,0},{20,4},{24,8},{28,12},{1,17},{... | collective-permute-start | bytes 786440 | tf_op jit(solution)/shard_map/ppermute | solution.py:589
  115.7 9.0 %collective-permute-start.43 = (bf16[512,256]{1,0:T(8,128)(2,1)S(1)}, bf16[512,256]{1,0:T(8,128)(2,1)S(1)}, u32[]{:S(2)}, u32[]{:S(2)}) collective-permute-start(bf16[512,256]{1,0:T(8,128)(2,1)S(1)} %constant_dynamic-update-slice_fusion.17), channel_id=1, source_target_pairs={{0,8},{4,12},{8,0},{12,4},{16,24},{20,28},{24,16},{28,20},{1,9},{5... | collective-permute-start | bytes 786440 | tf_op jit(solution)/shard_map/ppermute | solution.py:589
  116.8 9.8 %collective-permute-start.41 = (bf16[128,768]{1,0:T(8,128)(2,1)S(1)}, bf16[128,768]{1,0:T(8,128)(2,1)S(1)}, u32[]{:S(2)}, u32[]{:S(2)}) collective-permute-start(bf16[128,768]{1,0:T(8,128)(2,1)S(1)} %constant_dynamic-update-slice_fusion.21), channel_id=1, source_target_pairs={{0,8},{4,12},{8,0},{12,4},{16,24},{20,28},{24,16},{28,20},{1,9},{5... | collective-permute-start | bytes 589832 | tf_op jit(solution)/shard_map/ppermute | solution.py:589
  119.0 7.6 %collective-permute-start.42 = (bf16[128,896]{1,0:T(8,128)(2,1)S(1)}, bf16[128,896]{1,0:T(8,128)(2,1)S(1)}, u32[]{:S(2)}, u32[]{:S(2)}) collective-permute-start(bf16[128,896]{1,0:T(8,128)(2,1)S(1)} %constant_dynamic-update-slice_fusion.23), channel_id=1, source_target_pairs={{0,16},{4,20},{8,24},{12,28},{16,0},{20,4},{24,8},{28,12},{1,17},{... | collective-permute-start | bytes 688136 | tf_op jit(solution)/shard_map/ppermute | solution.py:589
  (25 other events, 119.6 us)
where the time goes:
time: 135 us; the launch traced here: 134 us
  starting transfers between devices  51.2 us (38%)
  Pallas kernels  47.4 us (35%)
  waiting for transfers between devices  22.8 us (17%)
  local copies, waits for them, and re-layouts  8.27 us (6%)
  other arithmetic  2.85 us (2%)
  between operations  2.07 us (2%)
    ppermute x42, starting transfers between devices, swap(): return lax.ppermute(value, axis, [(i, i ^ mask) for i in range(size)])  43 us
    ppermute x42, waiting for transfers between devices, swap(): return lax.ppermute(value, axis, [(i, i ^ mask) for i in range(size)])  18.6 us
    pallas_call x2, Pallas kernels, attention_backward(): pl.pallas_call(functools.partial(backward_kernel, parts, count, rows), gr...  10.7 us
    pallas_call x3, Pallas kernels, assemble(): pl.pallas_call(functools.partial(assemble_kernel, segments, mode, per), g...  8.93 us
    pallas_call x1, Pallas kernels, middle_part(): pl.pallas_call(functools.partial(middle_kernel, len(dys), rows), out_shap...  8.25 us
    ppermute x6, starting transfers between devices, deal(): got.append(lax.ppermute(pieces[j], 'seq', turn))  8.15 us
    pallas_call x1, Pallas kernels, attention_forward(): pl.pallas_call(functools.partial(forward_kernel, parts, wide, rows), grid...  7.02 us
    pallas_call x2, Pallas kernels, weight_grad(): pl.pallas_call(functools.partial(weight_grad_kernel, len(pairs), mode), i...  5.18 us
  transfers between devices with their start and end apart: 48, of which 20 were waited for; matrix products, arithmetic and copies ran while one was open for 5% of the time, Pallas kernels for 24%

commit v1 on v0

--- a/solution.py
+++ b/solution.py
@@ -14,8 +14,8 @@
 PIECES = 16
 AT_ONCE = 2
 SCHEDULE = (
-    "U", "D", "u", "b", "u", "b", "u", "d", "G", "u", "q", "d", "u", "L", "q", "d",
-    "u", "q", "d", "q", "u", "d", "O", "q", "d", "u", "q", "d", "q", "I", "u", "d",
+    "U", "D", "u", "b", "u", "b", "u", "d", "G", "u", "q", "d", "L", "u", "q", "d",
+    "u", "q", "d", "q", "u", "d", "q", "O", "d", "u", "q", "d", "I", "q", "u", "d",
     "q", "d", "q",
 )
 MODES = {"d": "xy", "u": "xy", "q": "xy"}

time: 135 us -> 135 us (level)
  transfers between devices with their start and end apart: 48 -> 48, of which waited for: 20 -> 19; matrix products, arithmetic and copies ran while one was open for 5% -> 5% of each run, Pallas kernels for 24% -> 24%
where the time goes in v1:
time: 135 us; the launch traced here: 134 us
  starting transfers between devices  50.1 us (37%)
  Pallas kernels  47.3 us (35%)
  waiting for transfers between devices  23.7 us (18%)
  local copies, waits for them, and re-layouts  8.27 us (6%)
  other arithmetic  2.82 us (2%)
  between operations  2.08 us (2%)
    ppermute x42, starting transfers between devices, swap(): return lax.ppermute(value, axis, [(i, i ^ mask) for i in range(size)])  41.9 us
    ppermute x42, waiting for transfers between devices, swap(): return lax.ppermute(value, axis, [(i, i ^ mask) for i in range(size)])  19.5 us
    pallas_call x2, Pallas kernels, attention_backward(): pl.pallas_call(functools.partial(backward_kernel, parts, count, rows), gr...  10.7 us
    pallas_call x3, Pallas kernels, assemble(): pl.pallas_call(functools.partial(assemble_kernel, segments, mode, per), g...  8.9 us
    pallas_call x1, Pallas kernels, middle_part(): pl.pallas_call(functools.partial(middle_kernel, len(dys), rows), out_shap...  8.25 us
    ppermute x6, starting transfers between devices, deal(): got.append(lax.ppermute(pieces[j], 'seq', turn))  8.15 us
    pallas_call x1, Pallas kernels, attention_forward(): pl.pallas_call(functools.partial(forward_kernel, parts, wide, rows), grid...  7.02 us
    pallas_call x2, Pallas kernels, weight_grad(): pl.pallas_call(functools.partial(weight_grad_kernel, len(pairs), mode), i...  5.18 us
  transfers between devices with their start and end apart: 48, of which 19 were waited for; matrix products, arithmetic and copies ran while one was open for 5% of the time, Pallas kernels for 24%

profile of v1, /device:TPU:0, one launch (start us, length us, event | category | flops | bytes accessed | tf_op | source)
XLA Modules:
  0.0 134.3 jit_solution(7249177193333549071)
XLA Ops:
  1.9 4.0 %collective-permute-start.2 = (bf16[128,512]{1,0:T(8,128)(2,1)S(1)}, bf16[128,512]{1,0:T(8,128)(2,1)S(1)}, u32[]{:S(2)}, u32[]{:S(2)}) collective-permute-start(bf16[128,512]{1,0:T(8,128)(2,1)S(1)} %get-tuple-element.317), channel_id=1, source_target_pairs={{0,24},{4,28},{8,16},{12,20},{16,8},{20,12},{24,0},{28,4},{1,25},{... | collective-permute-start | bytes 393224 | tf_op jit(solution)/shard_map/ppermute | solution.py:766
  8.2 1.9 %collective-permute-done.2.refs_3_ = bf16[128,512]{1,0:T(8,128)(2,1)S(1)} collective-permute-done((bf16[128,512]{1,0:T(8,128)(2,1)S(1)}, bf16[128,512]{1,0:T(8,128)(2,1)S(1)}, u32[]{:S(2)}, u32[]{:S(2)}) %collective-permute-start.2) | collective-permute-done | bytes 131104 | tf_op jit(solution)/shard_map/ppermute | solution.py:766
  10.1 2.2 %collective-permute-done.refs_1_ = bf16[128,512]{1,0:T(8,128)(2,1)S(1)} collective-permute-done((bf16[128,512]{1,0:T(8,128)(2,1)S(1)}, bf16[128,512]{1,0:T(8,128)(2,1)S(1)}, u32[]{:S(2)}, u32[]{:S(2)}) %collective-permute-start) | collective-permute-done | bytes 131104 | tf_op jit(solution)/shard_map/ppermute | solution.py:766
  17.6 1.6 %collective-permute-start.3 = (bf16[128,512]{1,0:T(8,128)(2,1)S(1)}, bf16[128,512]{1,0:T(8,128)(2,1)S(1)}, u32[]{:S(2)}, u32[]{:S(2)}) collective-permute-start(bf16[128,512]{1,0:T(8,128)(2,1)S(1)} %get-tuple-element.162), channel_id=1, source_target_pairs={{0,8},{4,12},{8,0},{12,4},{16,24},{20,28},{24,16},{28,20},{1,9},{5... | collective-permute-start | bytes 393224 | tf_op jit(solution)/shard_map/ppermute | solution.py:766
  21.3 7.0 %attention_forward.1 = (f32[512,512]{1,0:T(8,128)S(1)}, bf16[512,512]{1,0:T(8,128)(2,1)S(1)}) custom-call(bf16[512,512]{1,0:T(8,128)(2,1)S(1)} %get-tuple-element.166.refs_0_, bf16[512,1024]{1,0:T(8,128)(2,1)S(1)} %get-tuple-element.160.refs_1_.refs_3_.refs_4_.refs_6_, bf16[512,1024]{1,0:T(8,128)(2,1)S(1)} %collective-permute-done.6.refs_2_.refs_4_.refs_5_.refs_7_, ...), custom_call_target="tpu_custom_call" | custom-call | flops 1073741824 | bytes 2097152 | tf_op jit(solution)/shard_map/attention_forward/pallas_call | solution.py:177
  28.4 8.2 %middle_part.1 = (bf16[128,512]{1,0:T(8,128)(2,1)S(1)}, bf16[128,512]{1,0:T(8,128)(2,1)S(1)}, bf16[128,512]{1,0:T(8,128)(2,1)S(1)}, bf16[128,512]{1,0:T(8,128)(2...) custom-call(bf16[128,512]{1,0:T(8,128)(2,1)S(1)} %get-tuple-element., ...), custom_call_target="tpu_custom_call" | custom-call | flops 5637144576 | bytes 8388608 | tf_op jit(solution)/shard_map/middle_part/pallas_call | solution.py:354
  36.6 2.6 %grad_up_out.1 = (bf16[256,2560]{1,0:T(8,128)(2,1)S(1)}, bf16[256,2560]{1,0:T(8,128)(2,1)S(1)}) custom-call(s32[4]{0:T(128)S(1)} %pad_add_fusion.marks.refs_0_, bf16[512,512]{1,0:T(8,128)(2,1)S(1)} %get-tuple-element.175.refs_0_, bf16[512,2048]{1,0:T(8,128)(2,1)S(1)} %get-tuple-element.176.refs_1_, bf16[512,512]{1,0:T(8,128)(2,1)S(1)} %get-tuple-element.177.refs_2_, ...), custom_call_target="tpu_custom_call" | custom-call | flops 1342177280 | bytes 7864320 | tf_op jit(solution)/shard_map/grad_up_out/pallas_call | solution.py:427
  39.3 2.6 %grad_down.1 = (bf16[1024,512]{1,0:T(8,128)(2,1)S(1)}, bf16[1024,512]{1,0:T(8,128)(2,1)S(1)}) custom-call(s32[4]{0:T(128)S(1)} %pad_add_fusion.marks.refs_0_, bf16[512,2048]{1,0:T(8,128)(2,1)S(1)} %get-tuple-element.180.refs_0_, bf16[512,512]{1,0:T(8,128)(2,1)S(1)} %get-tuple-element.181.refs_1_), custom_call_target="tpu_custom_call" | custom-call | flops 1073741824 | bytes 6291456 | tf_op jit(solution)/shard_map/grad_down/pallas_call | solution.py:427
  42.9 1.5 %collective-permute-start.10 = (bf16[128,1280]{1,0:T(8,128)(2,1)S(1)}, bf16[128,1280]{1,0:T(8,128)(2,1)S(1)}, u32[]{:S(2)}, u32[]{:S(2)}) collective-permute-start(bf16[128,1280]{1,0:T(8,128)(2,1)S(1)} %get-tuple-element.305), channel_id=1, source_target_pairs={{0,16},{4,20},{8,24},{12,28},{16,0},{20,4},{24,8},{28,12},{1,17},{... | collective-permute-start | bytes 983048 | tf_op jit(solution)/shard_map/ppermute | solution.py:589
  45.9 5.4 %attention_backward.2 = (bf16[512,256]{1,0:T(8,128)(2,1)S(1)}, f32[512,512]{1,0:T(8,128)S(1)}, bf16[512,512]{1,0:T(8,128)(2,1)S(1)}) custom-call(bf16[512,512]{1,0:T(8,128)(2,1)S(1)} %get-tuple-element.166.refs_0_, bf16[512,512]{1,0:T(8,128)(2,1)S(1)} %get-tuple-element.198.refs_1_, bf16[512,512]{1,0:T(8,128)(2,1)S(1)} %get-tuple-element.189.refs_2_, ...), custom_call_target="tpu_custom_call" | custom-call | flops 1342177280 | bytes 1572864 | tf_op jit(solution)/shard_map/attention_backward/pallas_call | solution.py:258
  54.7 1.5 %collective-permute-start.12 = (bf16[64,1280]{1,0:T(8,128)(2,1)S(1)}, bf16[64,1280]{1,0:T(8,128)(2,1)S(1)}, u32[]{:S(2)}, u32[]{:S(2)}) collective-permute-start(bf16[64,1280]{1,0:T(8,128)(2,1)S(1)} %get-tuple-element.337), channel_id=1, source_target_pairs={{0,8},{4,12},{8,0},{12,4},{16,24},{20,28},{24,16},{28,20},{1,9},{5... | collective-permute-start | bytes 491528 | tf_op jit(solution)/shard_map/ppermute | solution.py:589
  56.3 5.4 %attention_backward.3 = (bf16[512,256]{1,0:T(8,128)(2,1)S(1)}, f32[512,512]{1,0:T(8,128)S(1)}, bf16[512,512]{1,0:T(8,128)(2,1)S(1)}) custom-call(bf16[512,512]{1,0:T(8,128)(2,1)S(1)} %get-tuple-element.166.refs_0_, bf16[512,512]{1,0:T(8,128)(2,1)S(1)} %get-tuple-element.198.refs_1_, bf16[512,512]{1,0:T(8,128)(2,1)S(1)} %get-tuple-element.189.refs_2_, ...), custom_call_target="tpu_custom_call" | custom-call | flops 1342177280 | bytes 1572864 | tf_op jit(solution)/shard_map/attention_backward/pallas_call | solution.py:258
  62.4 1.6 %collective-permute-start.18 = (bf16[32,2560]{1,0:T(8,128)(2,1)S(1)}, bf16[32,2560]{1,0:T(8,128)(2,1)S(1)}, u32[]{:S(2)}, u32[]{:S(2)}) collective-permute-start(bf16[32,2560]{1,0:T(8,128)(2,1)S(1)} %pad_maximum_fusion.2), channel_id=1, source_target_pairs={{0,1},{1,0},{2,3},{3,2},{4,5},{5,4},{6,7},{7,6},{8,9},{9,8},{10,11... | collective-permute-start | bytes 491528 | tf_op jit(solution)/shard_map/ppermute | solution.py:589
  66.6 3.0 %qkv_grad.1 = (bf16[512,1536]{1,0:T(8,128)(2,1)S(1)}, bf16[256,1664]{1,0:T(8,128)(2,1)S(1)}, bf16[256,1664]{1,0:T(8,128)(2,1)S(1)}) custom-call(s32[4]{0:T(128)S(1)} %pad_add_fusion.marks.refs_0_, bf16[512,512]{1,0:T(8,128)(2,1)S(1)} %copy-done.5, f32[12,512]{1,0:T(8,128)S(1)} %concatenate.140.refs_4_.refs_6_.refs_2_.small, bf16[512,1536]{1,0:T(8,128)(2,1)S(1)} %copy-done.3, ...), custom_call_target="tpu_custom_call" | custom-call | flops 805306368 | bytes 4718592 | tf_op jit(solution)/shard_map/qkv_grad/pallas_call | solution.py:481
  69.8 2.7 %collective-permute-start.23 = (bf16[32,2560]{1,0:T(8,128)(2,1)S(1)}, bf16[32,2560]{1,0:T(8,128)(2,1)S(1)}, u32[]{:S(2)}, u32[]{:S(2)}) collective-permute-start(bf16[32,2560]{1,0:T(8,128)(2,1)S(1)} %add_convert_fusion.10), channel_id=1, source_target_pairs={{0,2},{1,3},{2,0},{3,1},{4,6},{5,7},{6,4},{7,5},{8,10},{9,11},{10,... | collective-permute-start | bytes 491528 | tf_op jit(solution)/shard_map/ppermute | solution.py:589
  72.7 1.6 %collective-permute-start.21 = (bf16[128,768]{1,0:T(8,128)(2,1)S(1)}, bf16[128,768]{1,0:T(8,128)(2,1)S(1)}, u32[]{:S(2)}, u32[]{:S(2)}) collective-permute-start(bf16[128,768]{1,0:T(8,128)(2,1)S(1)} %get-tuple-element.316), channel_id=1, source_target_pairs={{0,8},{4,12},{8,0},{12,4},{16,24},{20,28},{24,16},{28,20},{1,9},{5... | collective-permute-start | bytes 589832 | tf_op jit(solution)/shard_map/ppermute | solution.py:589
  76.0 1.5 %collective-permute-start.20 = (bf16[256,512]{1,0:T(8,128)(2,1)S(1)}, bf16[256,512]{1,0:T(8,128)(2,1)S(1)}, u32[]{:S(2)}, u32[]{:S(2)}) collective-permute-start(bf16[256,512]{1,0:T(8,128)(2,1)S(1)} %maximum_maximum_fusion.5), channel_id=1, source_target_pairs={{0,8},{4,12},{8,0},{12,4},{16,24},{20,28},{24,16},{28,20},{1,9},{5... | collective-permute-start | bytes 786440 | tf_op jit(solution)/shard_map/ppermute | solution.py:589
  77.5 2.0 %collective-permute-start.19 = (bf16[256,512]{1,0:T(8,128)(2,1)S(1)}, bf16[256,512]{1,0:T(8,128)(2,1)S(1)}, u32[]{:S(2)}, u32[]{:S(2)}) collective-permute-start(bf16[256,512]{1,0:T(8,128)(2,1)S(1)} %fusion.22), channel_id=1, source_target_pairs={{0,16},{4,20},{8,24},{12,28},{16,0},{20,4},{24,8},{28,12},{1,17},{... | collective-permute-start | bytes 786440 | tf_op jit(solution)/shard_map/ppermute | solution.py:589
  84.3 1.8 %collective-permute-done.20 = bf16[256,512]{1,0:T(8,128)(2,1)S(1)} collective-permute-done((bf16[256,512]{1,0:T(8,128)(2,1)S(1)}, bf16[256,512]{1,0:T(8,128)(2,1)S(1)}, u32[]{:S(2)}, u32[]{:S(2)}) %collective-permute-start.20) | collective-permute-done | bytes 262176 | tf_op jit(solution)/shard_map/ppermute | solution.py:589
  86.1 2.3 %collective-permute-done.19 = bf16[256,512]{1,0:T(8,128)(2,1)S(1)} collective-permute-done((bf16[256,512]{1,0:T(8,128)(2,1)S(1)}, bf16[256,512]{1,0:T(8,128)(2,1)S(1)}, u32[]{:S(2)}, u32[]{:S(2)}) %collective-permute-start.19) | collective-permute-done | bytes 262176 | tf_op jit(solution)/shard_map/ppermute | solution.py:589
  92.4 1.7 %collective-permute-done.28 = bf16[128,512]{1,0:T(8,128)(2,1)S(1)} collective-permute-done((bf16[128,512]{1,0:T(8,128)(2,1)S(1)}, bf16[128,512]{1,0:T(8,128)(2,1)S(1)}, u32[]{:S(2)}, u32[]{:S(2)}) %collective-permute-start.28) | collective-permute-done | bytes 131104 | tf_op jit(solution)/shard_map/ppermute | solution.py:589
  94.1 3.2 %collective-permute-start.30 = (bf16[128,512]{1,0:T(8,128)(2,1)S(1)}, bf16[128,512]{1,0:T(8,128)(2,1)S(1)}, u32[]{:S(2)}, u32[]{:S(2)}) collective-permute-start(bf16[128,512]{1,0:T(8,128)(2,1)S(1)} %add_convert_fusion.14), channel_id=1, source_target_pairs={{0,2},{1,3},{2,0},{3,1},{4,6},{5,7},{6,4},{7,5},{8,10},{9,11},{10,... | collective-permute-start | bytes 393224 | tf_op jit(solution)/shard_map/ppermute | solution.py:589
  97.3 1.8 %collective-permute-start.29 = (bf16[32,1664]{1,0:T(8,128)(2,1)S(1)}, bf16[32,1664]{1,0:T(8,128)(2,1)S(1)}, u32[]{:S(2)}, u32[]{:S(2)}) collective-permute-start(bf16[32,1664]{1,0:T(8,128)(2,1)S(1)} %add_convert_fusion.19), channel_id=1, source_target_pairs={{0,2},{1,3},{2,0},{3,1},{4,6},{5,7},{6,4},{7,5},{8,10},{9,11},{10,... | collective-permute-start | bytes 319496 | tf_op jit(solution)/shard_map/ppermute | solution.py:589
  99.8 1.6 %collective-permute-start.34 = (bf16[128,1792]{1,0:T(8,128)(2,1)S(1)}, bf16[128,1792]{1,0:T(8,128)(2,1)S(1)}, u32[]{:S(2)}, u32[]{:S(2)}) collective-permute-start(bf16[128,1792]{1,0:T(8,128)(2,1)S(1)} %maximum_maximum_fusion.4), channel_id=1, source_target_pairs={{0,16},{4,20},{8,24},{12,28},{16,0},{20,4},{24,8},{28,12},{1,17},{... | collective-permute-start | bytes 1376264 | tf_op jit(solution)/shard_map/ppermute | solution.py:589
  101.3 1.7 %collective-permute-done.30 = bf16[128,512]{1,0:T(8,128)(2,1)S(1)} collective-permute-done((bf16[128,512]{1,0:T(8,128)(2,1)S(1)}, bf16[128,512]{1,0:T(8,128)(2,1)S(1)}, u32[]{:S(2)}, u32[]{:S(2)}) %collective-permute-start.30) | collective-permute-done | bytes 131104 | tf_op jit(solution)/shard_map/ppermute | solution.py:589
  106.2 2.0 %collective-permute-done.35 = bf16[128,512]{1,0:T(8,128)(2,1)S(1)} collective-permute-done((bf16[128,512]{1,0:T(8,128)(2,1)S(1)}, bf16[128,512]{1,0:T(8,128)(2,1)S(1)}, u32[]{:S(2)}, u32[]{:S(2)}) %collective-permute-start.35) | collective-permute-done | bytes 131104 | tf_op jit(solution)/shard_map/ppermute | solution.py:589
  113.7 1.9 %collective-permute-start.44 = (bf16[512,256]{1,0:T(8,128)(2,1)S(1)}, bf16[512,256]{1,0:T(8,128)(2,1)S(1)}, u32[]{:S(2)}, u32[]{:S(2)}) collective-permute-start(bf16[512,256]{1,0:T(8,128)(2,1)S(1)} %constant_dynamic-update-slice_fusion.19), channel_id=1, source_target_pairs={{0,16},{4,20},{8,24},{12,28},{16,0},{20,4},{24,8},{28,12},{1,17},{... | collective-permute-start | bytes 786440 | tf_op jit(solution)/shard_map/ppermute | solution.py:589
  118.8 1.6 %collective-permute-start.41 = (bf16[128,768]{1,0:T(8,128)(2,1)S(1)}, bf16[128,768]{1,0:T(8,128)(2,1)S(1)}, u32[]{:S(2)}, u32[]{:S(2)}) collective-permute-start(bf16[128,768]{1,0:T(8,128)(2,1)S(1)} %constant_dynamic-update-slice_fusion.21), channel_id=1, source_target_pairs={{0,8},{4,12},{8,0},{12,4},{16,24},{20,28},{24,16},{28,20},{1,9},{5... | collective-permute-start | bytes 589832 | tf_op jit(solution)/shard_map/ppermute | solution.py:589
  120.4 3.3 %assemble_up_out.1 = (f32[512,2048]{1,0:T(8,128)}, f32[512,512]{1,0:T(8,128)}) custom-call(s32[4]{0:T(128)S(1)} %pad_add_fusion.marks.refs_0_, bf16[256,2560]{1,0:T(8,128)(2,1)S(1)} %maximum_maximum_fusion.refs_0_, bf16[256,2560]{1,0:T(8,128)(2,1)S(1)} %collective-permute-done.45.refs_1_), custom_call_target="tpu_custom_call" | custom-call | flops 1310720 | bytes 7864320 | tf_op jit(solution)/shard_map/assemble_up_out/pallas_call | solution.py:548
  124.7 1.9 %collective-permute-done.41 = bf16[128,768]{1,0:T(8,128)(2,1)S(1)} collective-permute-done((bf16[128,768]{1,0:T(8,128)(2,1)S(1)}, bf16[128,768]{1,0:T(8,128)(2,1)S(1)}, u32[]{:S(2)}, u32[]{:S(2)}) %collective-permute-start.41) | collective-permute-done | bytes 196640 | tf_op jit(solution)/shard_map/ppermute | solution.py:589
  127.3 3.0 %assemble_down.1 = f32[2048,512]{1,0:T(8,128)} custom-call(s32[4]{0:T(128)S(1)} %pad_add_fusion.marks.refs_0_, bf16[1024,512]{1,0:T(8,128)(2,1)S(1)} %maximum_maximum_fusion.1.refs_0_, bf16[1024,512]{1,0:T(8,128)(2,1)S(1)} %collective-permute-done.47.refs_1_), custom_call_target="tpu_custom_call" | custom-call | flops 1048576 | bytes 6291456 | tf_op jit(solution)/shard_map/assemble_down/pallas_call | solution.py:548
  130.3 2.6 %assemble_qkv.1 = (f32[512,1536]{1,0:T(8,128)}, f32[512,128]{1,0:T(8,128)S(1)}) custom-call(s32[4]{0:T(128)S(1)} %pad_add_fusion.marks.refs_0_, bf16[256,1664]{1,0:T(8,128)(2,1)S(1)} %maximum_maximum_fusion.2.refs_0_, bf16[256,1664]{1,0:T(8,128)(2,1)S(1)} %collective-permute-done.46.refs_1_), custom_call_target="tpu_custom_call" | custom-call | flops 851968 | bytes 5111808 | tf_op jit(solution)/shard_map/assemble_qkv/pallas_call | solution.py:548
  (221 shorter events, 45.6 us)
Async XLA Ops:
  1.9 8.3 %collective-permute-start.2 = (bf16[128,512]{1,0:T(8,128)(2,1)S(1)}, bf16[128,512]{1,0:T(8,128)(2,1)S(1)}, u32[]{:S(2)}, u32[]{:S(2)}) collective-permute-start(bf16[128,512]{1,0:T(8,128)(2,1)S(1)} %get-tuple-element.317), channel_id=1, source_target_pairs={{0,24},{4,28},{8,16},{12,20},{16,8},{20,12},{24,0},{28,4},{1,25},{... | collective-permute-start | bytes 393224 | tf_op jit(solution)/shard_map/ppermute | solution.py:766
  17.6 10.7 %collective-permute-start.3 = (bf16[128,512]{1,0:T(8,128)(2,1)S(1)}, bf16[128,512]{1,0:T(8,128)(2,1)S(1)}, u32[]{:S(2)}, u32[]{:S(2)}) collective-permute-start(bf16[128,512]{1,0:T(8,128)(2,1)S(1)} %get-tuple-element.162), channel_id=1, source_target_pairs={{0,8},{4,12},{8,0},{12,4},{16,24},{20,28},{24,16},{28,20},{1,9},{5... | collective-permute-start | bytes 393224 | tf_op jit(solution)/shard_map/ppermute | solution.py:766
  19.2 9.1 %collective-permute-start.4 = (bf16[128,512]{1,0:T(8,128)(2,1)S(1)}, bf16[128,512]{1,0:T(8,128)(2,1)S(1)}, u32[]{:S(2)}, u32[]{:S(2)}) collective-permute-start(bf16[128,512]{1,0:T(8,128)(2,1)S(1)} %get-tuple-element.163), channel_id=1, source_target_pairs={{0,16},{4,20},{8,24},{12,28},{16,0},{20,4},{24,8},{28,12},{1,17},{... | collective-permute-start | bytes 393224 | tf_op jit(solution)/shard_map/ppermute | solution.py:766
  20.6 7.7 %collective-permute-start.5 = (bf16[128,512]{1,0:T(8,128)(2,1)S(1)}, bf16[128,512]{1,0:T(8,128)(2,1)S(1)}, u32[]{:S(2)}, u32[]{:S(2)}) collective-permute-start(bf16[128,512]{1,0:T(8,128)(2,1)S(1)} %get-tuple-element.164), channel_id=1, source_target_pairs={{0,24},{4,28},{8,16},{12,20},{16,8},{20,12},{24,0},{28,4},{1,25},{... | collective-permute-start | bytes 393224 | tf_op jit(solution)/shard_map/ppermute | solution.py:766
  41.9 22.1 %collective-permute-start.7 = (bf16[1024,512]{1,0:T(8,128)(2,1)S(1)}, bf16[1024,512]{1,0:T(8,128)(2,1)S(1)}, u32[]{:S(2)}, u32[]{:S(2)}) collective-permute-start(bf16[1024,512]{1,0:T(8,128)(2,1)S(1)} %get-tuple-element.183), channel_id=1, source_target_pairs={{0,4},{4,0},{8,12},{12,8},{16,20},{20,16},{24,28},{28,24},{1,5},{5... | collective-permute-start | bytes 3145736 | tf_op jit(solution)/shard_map/ppermute | solution.py:589
  42.9 9.7 %collective-permute-start.10 = (bf16[128,1280]{1,0:T(8,128)(2,1)S(1)}, bf16[128,1280]{1,0:T(8,128)(2,1)S(1)}, u32[]{:S(2)}, u32[]{:S(2)}) collective-permute-start(bf16[128,1280]{1,0:T(8,128)(2,1)S(1)} %get-tuple-element.305), channel_id=1, source_target_pairs={{0,16},{4,20},{8,24},{12,28},{16,0},{20,4},{24,8},{28,12},{1,17},{... | collective-permute-start | bytes 983048 | tf_op jit(solution)/shard_map/ppermute | solution.py:589
  44.4 9.4 %collective-permute-start.9 = (bf16[128,1280]{1,0:T(8,128)(2,1)S(1)}, bf16[128,1280]{1,0:T(8,128)(2,1)S(1)}, u32[]{:S(2)}, u32[]{:S(2)}) collective-permute-start(bf16[128,1280]{1,0:T(8,128)(2,1)S(1)} %get-tuple-element.306), channel_id=1, source_target_pairs={{0,8},{4,12},{8,0},{12,4},{16,24},{20,28},{24,16},{28,20},{1,9},{5... | collective-permute-start | bytes 983048 | tf_op jit(solution)/shard_map/ppermute | solution.py:589
  53.9 8.3 %collective-permute-start.11 = (bf16[64,1280]{1,0:T(8,128)(2,1)S(1)}, bf16[64,1280]{1,0:T(8,128)(2,1)S(1)}, u32[]{:S(2)}, u32[]{:S(2)}) collective-permute-start(bf16[64,1280]{1,0:T(8,128)(2,1)S(1)} %get-tuple-element.339), channel_id=1, source_target_pairs={{0,16},{4,20},{8,24},{12,28},{16,0},{20,4},{24,8},{28,12},{1,17},{... | collective-permute-start | bytes 491528 | tf_op jit(solution)/shard_map/ppermute | solution.py:589
  54.7 7.5 %collective-permute-start.12 = (bf16[64,1280]{1,0:T(8,128)(2,1)S(1)}, bf16[64,1280]{1,0:T(8,128)(2,1)S(1)}, u32[]{:S(2)}, u32[]{:S(2)}) collective-permute-start(bf16[64,1280]{1,0:T(8,128)(2,1)S(1)} %get-tuple-element.337), channel_id=1, source_target_pairs={{0,8},{4,12},{8,0},{12,4},{16,24},{20,28},{24,16},{28,20},{1,9},{5... | collective-permute-start | bytes 491528 | tf_op jit(solution)/shard_map/ppermute | solution.py:589
  56.2 10.4 %collective-permute-start.15 = (bf16[512,512]{1,0:T(8,128)(2,1)S(1)}, bf16[512,512]{1,0:T(8,128)(2,1)S(1)}, u32[]{:S(2)}, u32[]{:S(2)}) collective-permute-start(bf16[512,512]{1,0:T(8,128)(2,1)S(1)} %get-tuple-element.193), channel_id=1, source_target_pairs={{0,4},{4,0},{8,12},{12,8},{16,20},{20,16},{24,28},{28,24},{1,5},{5... | collective-permute-start | bytes 1572872 | tf_op jit(solution)/shard_map/ppermute | solution.py:589
  62.4 7.4 %collective-permute-start.18 = (bf16[32,2560]{1,0:T(8,128)(2,1)S(1)}, bf16[32,2560]{1,0:T(8,128)(2,1)S(1)}, u32[]{:S(2)}, u32[]{:S(2)}) collective-permute-start(bf16[32,2560]{1,0:T(8,128)(2,1)S(1)} %pad_maximum_fusion.2), channel_id=1, source_target_pairs={{0,1},{1,0},{2,3},{3,2},{4,5},{5,4},{6,7},{7,6},{8,9},{9,8},{10,11... | collective-permute-start | bytes 491528 | tf_op jit(solution)/shard_map/ppermute | solution.py:589
  64.4 10.8 %collective-permute-start.13 = (bf16[512,384]{1,0:T(8,128)(2,1)S(1)}, bf16[512,384]{1,0:T(8,128)(2,1)S(1)}, u32[]{:S(2)}, u32[]{:S(2)}) collective-permute-start(bf16[512,384]{1,0:T(8,128)(2,1)S(1)} %fusion.13), channel_id=1, source_target_pairs={{0,8},{4,12},{8,0},{12,4},{16,24},{20,28},{24,16},{28,20},{1,9},{5... | collective-permute-start | bytes 1179656 | tf_op jit(solution)/shard_map/ppermute | solution.py:589
  65.1 10.6 %collective-permute-start.14 = (bf16[512,384]{1,0:T(8,128)(2,1)S(1)}, bf16[512,384]{1,0:T(8,128)(2,1)S(1)}, u32[]{:S(2)}, u32[]{:S(2)}) collective-permute-start(bf16[512,384]{1,0:T(8,128)(2,1)S(1)} %fusion.19), channel_id=1, source_target_pairs={{0,16},{4,20},{8,24},{12,28},{16,0},{20,4},{24,8},{28,12},{1,17},{... | collective-permute-start | bytes 1179656 | tf_op jit(solution)/shard_map/ppermute | solution.py:589
  69.8 11.1 %collective-permute-start.23 = (bf16[32,2560]{1,0:T(8,128)(2,1)S(1)}, bf16[32,2560]{1,0:T(8,128)(2,1)S(1)}, u32[]{:S(2)}, u32[]{:S(2)}) collective-permute-start(bf16[32,2560]{1,0:T(8,128)(2,1)S(1)} %add_convert_fusion.10), channel_id=1, source_target_pairs={{0,2},{1,3},{2,0},{3,1},{4,6},{5,7},{6,4},{7,5},{8,10},{9,11},{10,... | collective-permute-start | bytes 491528 | tf_op jit(solution)/shard_map/ppermute | solution.py:589
  72.7 8.7 %collective-permute-start.21 = (bf16[128,768]{1,0:T(8,128)(2,1)S(1)}, bf16[128,768]{1,0:T(8,128)(2,1)S(1)}, u32[]{:S(2)}, u32[]{:S(2)}) collective-permute-start(bf16[128,768]{1,0:T(8,128)(2,1)S(1)} %get-tuple-element.316), channel_id=1, source_target_pairs={{0,8},{4,12},{8,0},{12,4},{16,24},{20,28},{24,16},{28,20},{1,9},{5... | collective-permute-start | bytes 589832 | tf_op jit(solution)/shard_map/ppermute | solution.py:589
  74.3 8.5 %collective-permute-start.22 = (bf16[128,896]{1,0:T(8,128)(2,1)S(1)}, bf16[128,896]{1,0:T(8,128)(2,1)S(1)}, u32[]{:S(2)}, u32[]{:S(2)}) collective-permute-start(bf16[128,896]{1,0:T(8,128)(2,1)S(1)} %get-tuple-element.314), channel_id=1, source_target_pairs={{0,16},{4,20},{8,24},{12,28},{16,0},{20,4},{24,8},{28,12},{1,17},{... | collective-permute-start | bytes 688136 | tf_op jit(solution)/shard_map/ppermute | solution.py:589
  76.0 10.2 %collective-permute-start.20 = (bf16[256,512]{1,0:T(8,128)(2,1)S(1)}, bf16[256,512]{1,0:T(8,128)(2,1)S(1)}, u32[]{:S(2)}, u32[]{:S(2)}) collective-permute-start(bf16[256,512]{1,0:T(8,128)(2,1)S(1)} %maximum_maximum_fusion.5), channel_id=1, source_target_pairs={{0,8},{4,12},{8,0},{12,4},{16,24},{20,28},{24,16},{28,20},{1,9},{5... | collective-permute-start | bytes 786440 | tf_op jit(solution)/shard_map/ppermute | solution.py:589
  77.5 11.0 %collective-permute-start.19 = (bf16[256,512]{1,0:T(8,128)(2,1)S(1)}, bf16[256,512]{1,0:T(8,128)(2,1)S(1)}, u32[]{:S(2)}, u32[]{:S(2)}) collective-permute-start(bf16[256,512]{1,0:T(8,128)(2,1)S(1)} %fusion.22), channel_id=1, source_target_pairs={{0,16},{4,20},{8,24},{12,28},{16,0},{20,4},{24,8},{28,12},{1,17},{... | collective-permute-start | bytes 786440 | tf_op jit(solution)/shard_map/ppermute | solution.py:589
  80.9 8.2 %collective-permute-start.26 = (bf16[32,2560]{1,0:T(8,128)(2,1)S(1)}, bf16[32,2560]{1,0:T(8,128)(2,1)S(1)}, u32[]{:S(2)}, u32[]{:S(2)}) collective-permute-start(bf16[32,2560]{1,0:T(8,128)(2,1)S(1)} %add_convert_fusion.9), channel_id=1, source_target_pairs={{0,1},{1,0},{2,3},{3,2},{4,5},{5,4},{6,7},{7,6},{8,9},{9,8},{10,11... | collective-permute-start | bytes 491528 | tf_op jit(solution)/shard_map/ppermute | solution.py:589
  82.9 8.2 %collective-permute-start.24 = (bf16[64,768]{1,0:T(8,128)(2,1)S(1)}, bf16[64,768]{1,0:T(8,128)(2,1)S(1)}, u32[]{:S(2)}, u32[]{:S(2)}) collective-permute-start(bf16[64,768]{1,0:T(8,128)(2,1)S(1)} %get-tuple-element.362), channel_id=1, source_target_pairs={{0,16},{4,20},{8,24},{12,28},{16,0},{20,4},{24,8},{28,12},{1,17},{... | collective-permute-start | bytes 294920 | tf_op jit(solution)/shard_map/ppermute | solution.py:589
  83.7 7.5 %collective-permute-start.25 = (bf16[64,896]{1,0:T(8,128)(2,1)S(1)}, bf16[64,896]{1,0:T(8,128)(2,1)S(1)}, u32[]{:S(2)}, u32[]{:S(2)}) collective-permute-start(bf16[64,896]{1,0:T(8,128)(2,1)S(1)} %get-tuple-element.360), channel_id=1, source_target_pairs={{0,8},{4,12},{8,0},{12,4},{16,24},{20,28},{24,16},{28,20},{1,9},{5... | collective-permute-start | bytes 344072 | tf_op jit(solution)/shard_map/ppermute | solution.py:589
  89.4 9.7 %collective-permute-start.32 = (bf16[64,2304]{1,0:T(8,128)(2,1)S(1)}, bf16[64,2304]{1,0:T(8,128)(2,1)S(1)}, u32[]{:S(2)}, u32[]{:S(2)}) collective-permute-start(bf16[64,2304]{1,0:T(8,128)(2,1)S(1)} %get-tuple-element.373), channel_id=1, source_target_pairs={{0,8},{4,12},{8,0},{12,4},{16,24},{20,28},{24,16},{28,20},{1,9},{5... | collective-permute-start | bytes 884744 | tf_op jit(solution)/shard_map/ppermute | solution.py:589
  90.0 9.1 %collective-permute-start.31 = (bf16[64,2304]{1,0:T(8,128)(2,1)S(1)}, bf16[64,2304]{1,0:T(8,128)(2,1)S(1)}, u32[]{:S(2)}, u32[]{:S(2)}) collective-permute-start(bf16[64,2304]{1,0:T(8,128)(2,1)S(1)} %get-tuple-element.374), channel_id=1, source_target_pairs={{0,16},{4,20},{8,24},{12,28},{16,0},{20,4},{24,8},{28,12},{1,17},{... | collective-permute-start | bytes 884744 | tf_op jit(solution)/shard_map/ppermute | solution.py:589
  94.1 9.0 %collective-permute-start.30 = (bf16[128,512]{1,0:T(8,128)(2,1)S(1)}, bf16[128,512]{1,0:T(8,128)(2,1)S(1)}, u32[]{:S(2)}, u32[]{:S(2)}) collective-permute-start(bf16[128,512]{1,0:T(8,128)(2,1)S(1)} %add_convert_fusion.14), channel_id=1, source_target_pairs={{0,2},{1,3},{2,0},{3,1},{4,6},{5,7},{6,4},{7,5},{8,10},{9,11},{10,... | collective-permute-start | bytes 393224 | tf_op jit(solution)/shard_map/ppermute | solution.py:589
  97.3 7.8 %collective-permute-start.29 = (bf16[32,1664]{1,0:T(8,128)(2,1)S(1)}, bf16[32,1664]{1,0:T(8,128)(2,1)S(1)}, u32[]{:S(2)}, u32[]{:S(2)}) collective-permute-start(bf16[32,1664]{1,0:T(8,128)(2,1)S(1)} %add_convert_fusion.19), channel_id=1, source_target_pairs={{0,2},{1,3},{2,0},{3,1},{4,6},{5,7},{6,4},{7,5},{8,10},{9,11},{10,... | collective-permute-start | bytes 319496 | tf_op jit(solution)/shard_map/ppermute | solution.py:589
  99.2 10.9 %collective-permute-start.33 = (bf16[128,1792]{1,0:T(8,128)(2,1)S(1)}, bf16[128,1792]{1,0:T(8,128)(2,1)S(1)}, u32[]{:S(2)}, u32[]{:S(2)}) collective-permute-start(bf16[128,1792]{1,0:T(8,128)(2,1)S(1)} %maximum_maximum_fusion.3), channel_id=1, source_target_pairs={{0,8},{4,12},{8,0},{12,4},{16,24},{20,28},{24,16},{28,20},{1,9},{5... | collective-permute-start | bytes 1376264 | tf_op jit(solution)/shard_map/ppermute | solution.py:589
  99.8 10.7 %collective-permute-start.34 = (bf16[128,1792]{1,0:T(8,128)(2,1)S(1)}, bf16[128,1792]{1,0:T(8,128)(2,1)S(1)}, u32[]{:S(2)}, u32[]{:S(2)}) collective-permute-start(bf16[128,1792]{1,0:T(8,128)(2,1)S(1)} %maximum_maximum_fusion.4), channel_id=1, source_target_pairs={{0,16},{4,20},{8,24},{12,28},{16,0},{20,4},{24,8},{28,12},{1,17},{... | collective-permute-start | bytes 1376264 | tf_op jit(solution)/shard_map/ppermute | solution.py:589
  110.7 9.7 %collective-permute-start.45 = (bf16[256,2560]{1,0:T(8,128)(2,1)S(1)}, bf16[256,2560]{1,0:T(8,128)(2,1)S(1)}, u32[]{:S(2)}, u32[]{:S(2)}) collective-permute-start(bf16[256,2560]{1,0:T(8,128)(2,1)S(1)} %maximum_maximum_fusion.refs_0_), channel_id=1, source_target_pairs={{0,4},{4,0},{8,12},{12,8},{16,20},{20,16},{24,28},{28,24},{1,5},{5... | collective-permute-start | bytes 3932168 | tf_op jit(solution)/shard_map/ppermute | solution.py:589
  113.7 10.0 %collective-permute-start.44 = (bf16[512,256]{1,0:T(8,128)(2,1)S(1)}, bf16[512,256]{1,0:T(8,128)(2,1)S(1)}, u32[]{:S(2)}, u32[]{:S(2)}) collective-permute-start(bf16[512,256]{1,0:T(8,128)(2,1)S(1)} %constant_dynamic-update-slice_fusion.19), channel_id=1, source_target_pairs={{0,16},{4,20},{8,24},{12,28},{16,0},{20,4},{24,8},{28,12},{1,17},{... | collective-permute-start | bytes 786440 | tf_op jit(solution)/shard_map/ppermute | solution.py:589
  115.7 8.8 %collective-permute-start.43 = (bf16[512,256]{1,0:T(8,128)(2,1)S(1)}, bf16[512,256]{1,0:T(8,128)(2,1)S(1)}, u32[]{:S(2)}, u32[]{:S(2)}) collective-permute-start(bf16[512,256]{1,0:T(8,128)(2,1)S(1)} %constant_dynamic-update-slice_fusion.17), channel_id=1, source_target_pairs={{0,8},{4,12},{8,0},{12,4},{16,24},{20,28},{24,16},{28,20},{1,9},{5... | collective-permute-start | bytes 786440 | tf_op jit(solution)/shard_map/ppermute | solution.py:589
  117.4 9.2 %collective-permute-start.42 = (bf16[128,896]{1,0:T(8,128)(2,1)S(1)}, bf16[128,896]{1,0:T(8,128)(2,1)S(1)}, u32[]{:S(2)}, u32[]{:S(2)}) collective-permute-start(bf16[128,896]{1,0:T(8,128)(2,1)S(1)} %constant_dynamic-update-slice_fusion.23), channel_id=1, source_target_pairs={{0,16},{4,20},{8,24},{12,28},{16,0},{20,4},{24,8},{28,12},{1,17},{... | collective-permute-start | bytes 688136 | tf_op jit(solution)/shard_map/ppermute | solution.py:589
  118.8 7.8 %collective-permute-start.41 = (bf16[128,768]{1,0:T(8,128)(2,1)S(1)}, bf16[128,768]{1,0:T(8,128)(2,1)S(1)}, u32[]{:S(2)}, u32[]{:S(2)}) collective-permute-start(bf16[128,768]{1,0:T(8,128)(2,1)S(1)} %constant_dynamic-update-slice_fusion.21), channel_id=1, source_target_pairs={{0,8},{4,12},{8,0},{12,4},{16,24},{20,28},{24,16},{28,20},{1,9},{5... | collective-permute-start | bytes 589832 | tf_op jit(solution)/shard_map/ppermute | solution.py:589
  (25 other events, 120.5 us)
